TPU v7x, 256 devices: a whole 4x4x8 slice. The times are simulated.
256 devices in a mesh: ctx: 16 (over x_lo, z), tp: 16 (over y, x_hi, core).
Axes of the slice: x: 4 (x_hi: 2, x_lo: 2; x = x_hi * 2 + x_lo), y: 4, z: 8, core: 2. Of those that a mesh axis runs over, the one named last changes fastest.
Arguments:
- queries: bfloat16 [1024, 128, 128], P('ctx', 'tp'), may hold values from -400 to 400
- cache_keys: bfloat16 [8, 32768, 128], P(None, 'ctx'), may hold values from -6 to 6
- cache_values: bfloat16 [8, 32768, 128], P(None, 'ctx'), may hold values from -12 to 12
- span_keys: bfloat16 [8, 1024, 128], P(None, 'ctx'), may hold values from -3.6 to 3.6
- span_values: bfloat16 [8, 1024, 128], P(None, 'ctx'), may hold values from -12 to 12
- span_start: int32 [1], replicated, may hold values from 8192 to 15360
- cache_lengths: int32 [16], P('ctx'), may hold values from 1 to 2048, 16384 in all
- out_weight: bfloat16 [16384, 16384], P('tp', 'ctx'), may hold values from -0.046875 to 0.046875
Outputs:
- attended: bfloat16 [1024, 128, 128], P('ctx', 'tp')
- projected: bfloat16 [1024, 16384], P('tp', 'ctx')
All inputs are finite; a program needn't handle non-finite values. No bound on the sum of `cache_lengths` on one device may be relied on, other than what follows from the above.
Results may differ from a plain program's by a relative error of at most 0.019.
Values may be sent and summed in bfloat16 or wider, within the bound.
No kernel may reach another device: no remote copies, remote signals or barrier semaphores. Data moves between devices by JAX's collectives and lax.ppermute only.
A program may use at most 128 MiB of HBM per device.

v0:
```python
import jax
import jax.numpy as jnp
from jax import lax
from jax.sharding import PartitionSpec as P

H = 128
KVH = 8


NEG_FILL = -1e30


def carried_in(part, axis, combine, identity):
    place = lax.axis_index(axis)
    gathered = lax.all_gather(part, axis)
    state = jnp.zeros_like(part) + jnp.asarray(identity, part.dtype)

    def one(lap, state):
        return combine(state, lax.dynamic_index_in_dim(gathered, lap, 0, False))

    return lax.fori_loop(0, place, one, state)


def from_behind(block, axis, distance):
    devices = range(lax.axis_size(axis))
    route = [((i - distance) % len(devices), i) for i in devices]
    return lax.ppermute(block, axis, route)


def fresh_state(row_count, kv_count, per_head, head_dim):
    return (
        jnp.zeros((row_count, kv_count, per_head, head_dim), jnp.float32),
        jnp.full((row_count, kv_count, per_head), NEG_FILL, jnp.float32),
        jnp.zeros((row_count, kv_count, per_head), jnp.float32),
    )


def absorb(state, query_grid, key_tile, value_tile, allowed, score_scale):
    output_sum, peaks, totals = state
    scores = (
        jnp.einsum("rgpd,gkd->rgpk", query_grid, key_tile, preferred_element_type=jnp.float32)
        * score_scale
    )
    scores = jnp.where(allowed, scores, NEG_FILL)
    new_peak = jnp.maximum(peaks, jnp.max(scores, axis=-1))
    rescale = jnp.exp(peaks - new_peak)
    weights = jnp.where(allowed, jnp.exp(scores - new_peak[..., None]), 0.0)
    totals = totals * rescale + jnp.sum(weights, axis=-1)
    output_sum = output_sum * rescale[..., None] + jnp.einsum(
        "rgpk,gkd->rgpd",
        weights.astype(jnp.bfloat16),
        value_tile,
        preferred_element_type=jnp.float32,
    )
    return (output_sum, new_peak, totals)


def own_block(state, query_grid, row_first, key_block, value_block, score_scale):
    row_index = row_first + jnp.arange(query_grid.shape[0], dtype=jnp.int32)
    key_index = jnp.arange(key_block.shape[1], dtype=jnp.int32)
    allowed = (key_index[None, :] <= row_index[:, None])[:, None, None, :]
    return absorb(state, query_grid, key_block, value_block, allowed, score_scale)


def merge_sources(output_sum, peaks, totals):
    overall = jnp.max(peaks, axis=0)
    factor = jnp.exp(peaks - overall)
    return (jnp.sum(output_sum * factor[..., None], axis=0), jnp.sum(totals * factor, axis=0))


def local(
    queries, cache_keys, cache_values, span_keys, span_values, span_start, cache_lengths, out_weight
):
    query_rows, head_count, head_dim = queries.shape
    ctx_count = lax.axis_size("ctx")
    ctx_index = lax.axis_index("ctx")
    tp_index = lax.axis_index("tp")
    group_size = H // KVH
    kv_count = max(1, head_count // group_size)
    per_head = head_count // kv_count
    kv_first = tp_index * head_count // group_size
    score_scale = head_dim ** (-0.5)
    cache_here = lax.dynamic_slice_in_dim(cache_keys, kv_first, kv_count, 0)
    values_here = lax.dynamic_slice_in_dim(cache_values, kv_first, kv_count, 0)
    span_here = lax.dynamic_slice_in_dim(span_keys, kv_first, kv_count, 0)
    span_vals = lax.dynamic_slice_in_dim(span_values, kv_first, kv_count, 0)
    cache_len = cache_keys.shape[1]
    tile_len = min(512, cache_len)
    offset = carried_in(
        cache_lengths, "ctx", lambda earlier, later: earlier + later, jnp.zeros((1,), jnp.int32)
    )
    live_count = jnp.clip(span_start[0] - offset[0], 0, cache_lengths[0])
    tiles_live = (live_count + tile_len - 1) // tile_len

    def cache_pass(state, query_grid):

        def tile_step(tile_index, carried):
            tile_first = tile_index * tile_len
            key_tile = lax.dynamic_slice_in_dim(cache_here, tile_first, tile_len, 1)
            value_tile = lax.dynamic_slice_in_dim(values_here, tile_first, tile_len, 1)
            allowed = (tile_first + jnp.arange(tile_len, dtype=jnp.int32) < live_count)[
                None, None, None, :
            ]
            return absorb(carried, query_grid, key_tile, value_tile, allowed, score_scale)

        return lax.fori_loop(jnp.int32(0), tiles_live, tile_step, state)

    home_grid = queries.reshape(query_rows, kv_count, per_head, head_dim)
    home_first = ctx_index * query_rows

    def cycle_step(step_index, carried):
        query_grid = carried[0]
        state = cache_pass((carried[1], carried[2], carried[3]), query_grid)
        moved_query = from_behind(query_grid, "ctx", 1)
        moved_state = from_behind((state[0], state[1], state[2]), "ctx", 1)
        return (moved_query, moved_state[0], moved_state[1], moved_state[2])

    finished = lax.fori_loop(
        0,
        ctx_count,
        cycle_step,
        (home_grid,) + fresh_state(query_rows, kv_count, per_head, head_dim),
    )
    sources = (finished[1][None], finished[2][None], finished[3][None])
    own_state = own_block(
        fresh_state(query_rows, kv_count, per_head, head_dim),
        home_grid,
        home_first,
        lax.all_gather(span_here, "ctx", axis=1, tiled=True),
        lax.all_gather(span_vals, "ctx", axis=1, tiled=True),
        score_scale,
    )
    sources = tuple(
        (jnp.concatenate([sources[member], own_state[member][None]], axis=0) for member in range(3))
    )
    merged_sum, merged_total = merge_sources(sources[0], sources[1], sources[2])
    attended = (
        (merged_sum / merged_total[..., None])
        .reshape(query_rows, head_count, head_dim)
        .astype(jnp.bfloat16)
    )
    flat_rows = attended.reshape(query_rows, head_count * head_dim)
    every_row = lax.all_gather(flat_rows, "ctx", axis=0, tiled=True)
    projected = lax.psum_scatter(
        jnp.dot(every_row, out_weight, preferred_element_type=jnp.float32).astype(jnp.bfloat16),
        "tp",
        scatter_dimension=0,
        tiled=True,
    )
    return (attended, projected)


def solution(mesh):
    return jax.shard_map(
        local,
        mesh=mesh,
        in_specs=(
            P("ctx", "tp", None),
            P(None, "ctx", None),
            P(None, "ctx", None),
            P(None, "ctx", None),
            P(None, "ctx", None),
            P(),
            P("ctx"),
            P("tp", "ctx"),
        ),
        out_specs=(P("ctx", "tp", None), P("tp", "ctx")),
        check_vma=False,
    )
```

profile of v0, /device:TPU:1, one launch (start us, length us, event | category | flops | bytes accessed | tf_op | source)
XLA Modules:
  0.0 550.5 jit_solution(12015539269954729367)
XLA Ops:
  10.7 16.6 %all-reduce = s32[16]{0:T(128)S(1)} all-reduce(s32[16]{0:T(128)S(1)} %dynamic-update-slice), channel_id=2, replica_groups=mesh['ctx'=16,'tp'=16] {'ctx'}, use_global_device_ids=true, to_apply=%add | all-reduce | flops 16 | bytes 128
  30.4 44.7 %all_gather.18 = bf16[1,1024,128]{2,1,0:T(8,128)(2,1)} all-gather(bf16[1,64,128]{2,1,0:T(8,128)(2,1)S(1)} %constant_dynamic-slice_fusion.1), channel_id=1, replica_groups=mesh['ctx'=16,'tp'=16] {'ctx'}, dimensions={1}, use_global_device_ids=true | all-gather | bytes 278528 | tf_op jit(solution)/shard_map/all_gather | solution.py:130
  75.2 23.9 %all_gather.17 = bf16[1,1024,128]{2,1,0:T(8,128)(2,1)S(1)} all-gather(bf16[1,64,128]{2,1,0:T(8,128)(2,1)S(1)} %constant_dynamic-slice_fusion.2), channel_id=1, replica_groups=mesh['ctx'=16,'tp'=16] {'ctx'}, dimensions={1}, use_global_device_ids=true | all-gather | bytes 278528 | tf_op jit(solution)/shard_map/all_gather | solution.py:129
  102.9 244.8 %while.42 = (s32[]{:T(128)}, bf16[64,1,8,128]{3,0,2,1:T(8,128)(2,1)}, f32[64,1,8,128]{3,0,2,1:T(8,128)S(1)}, f32[64,1,8]{0,2,1:T(8,128)S(1)}, f32[64,1,8]{0,2,1:...) while((s32[]{:T(128)}, ...), condition=%wide.region_7.8_spmd, body=%wide.region_2.7_spmd.sunk | while | flops 136710656 | bytes 6486616 | solution.py:118
  108.9 6.4 %collective-permute-done.3 = f32[64,1,8]{0,2,1:T(8,128)S(1)} collective-permute-done((f32[64,1,8]{0,2,1:T(8,128)S(1)}, f32[64,1,8]{0,2,1:T(8,128)S(1)}, u32[]{:S(2)}, u32[]{:S(2)}) %collective-permute-start.3) | collective-permute-done | bytes 2080 | tf_op jit(solution)/shard_map/while/body/eval_jaxpr/ppermute | solution.py:27
  124.0 5.5 collective-permute-done.3
  133.9 2.7 collective-permute-start
  136.7 4.3 collective-permute-start.2
  148.3 2.9 collective-permute-start
  151.3 5.8 %collective-permute-start.2 = (f32[64,1,8]{0,2,1:T(8,128)S(1)}, f32[64,1,8]{0,2,1:T(8,128)S(1)}, u32[]{:S(2)}, u32[]{:S(2)}) collective-permute-start(f32[64,1,8]{0,2,1:T(8,128)S(1)} %get-tuple-element.343), channel_id=1, source_target_pairs={{240,0},{0,16},{16,32},{32,48},{48,64},{64,80},{80,96},{96,112},{1... | collective-permute-start | bytes 6152 | tf_op jit(solution)/shard_map/while/body/eval_jaxpr/ppermute | solution.py:27
  164.3 2.8 collective-permute-start
  167.3 5.1 collective-permute-start.2
  179.7 2.9 collective-permute-start
  182.6 4.4 collective-permute-start.2
  196.5 5.3 collective-permute-start.2
  211.2 5.3 collective-permute-start.2
  225.9 5.3 collective-permute-start.2
  240.7 5.3 collective-permute-start.2
  255.4 5.3 collective-permute-start.2
  270.1 5.5 %collective-permute-start.2 = (f32[64,1,8]{0,2,1:T(8,128)S(1)}, f32[64,1,8]{0,2,1:T(8,128)S(1)}, u32[]{:S(2)}, u32[]{:S(2)}) collective-permute-start(f32[64,1,8]{0,2,1:T(8,128)S(1)} %get-tuple-element.343), channel_id=1, source_target_pairs={{240,0},{0,16},{16,32},{32,48},{48,64},{64,80},{80,96},{96,112},{1... | collective-permute-start | bytes 6152 | tf_op jit(solution)/shard_map/while/body/eval_jaxpr/ppermute | solution.py:27
  282.5 3.1 collective-permute-start
  286.1 5.6 %collective-permute-start.2 = (f32[64,1,8]{0,2,1:T(8,128)S(1)}, f32[64,1,8]{0,2,1:T(8,128)S(1)}, u32[]{:S(2)}, u32[]{:S(2)}) collective-permute-start(f32[64,1,8]{0,2,1:T(8,128)S(1)} %get-tuple-element.343), channel_id=1, source_target_pairs={{240,0},{0,16},{16,32},{32,48},{48,64},{64,80},{80,96},{96,112},{1... | collective-permute-start | bytes 6152 | tf_op jit(solution)/shard_map/while/body/eval_jaxpr/ppermute | solution.py:27
  298.4 3.7 collective-permute-start
  303.1 5.6 %collective-permute-start.2 = (f32[64,1,8]{0,2,1:T(8,128)S(1)}, f32[64,1,8]{0,2,1:T(8,128)S(1)}, u32[]{:S(2)}, u32[]{:S(2)}) collective-permute-start(f32[64,1,8]{0,2,1:T(8,128)S(1)} %get-tuple-element.343), channel_id=1, source_target_pairs={{240,0},{0,16},{16,32},{32,48},{48,64},{64,80},{80,96},{96,112},{1... | collective-permute-start | bytes 6152 | tf_op jit(solution)/shard_map/while/body/eval_jaxpr/ppermute | solution.py:27
  315.7 4.3 collective-permute-start
  321.2 5.6 %collective-permute-start.2 = (f32[64,1,8]{0,2,1:T(8,128)S(1)}, f32[64,1,8]{0,2,1:T(8,128)S(1)}, u32[]{:S(2)}, u32[]{:S(2)}) collective-permute-start(f32[64,1,8]{0,2,1:T(8,128)S(1)} %get-tuple-element.343), channel_id=1, source_target_pairs={{240,0},{0,16},{16,32},{32,48},{48,64},{64,80},{80,96},{96,112},{1... | collective-permute-start | bytes 6152 | tf_op jit(solution)/shard_map/while/body/eval_jaxpr/ppermute | solution.py:27
  333.6 3.8 collective-permute-start
  337.4 2.7 collective-permute-start.3
  340.0 5.9 %collective-permute-start.2 = (f32[64,1,8]{0,2,1:T(8,128)S(1)}, f32[64,1,8]{0,2,1:T(8,128)S(1)}, u32[]{:S(2)}, u32[]{:S(2)}) collective-permute-start(f32[64,1,8]{0,2,1:T(8,128)S(1)} %get-tuple-element.343), channel_id=1, source_target_pairs={{240,0},{0,16},{16,32},{32,48},{48,64},{64,80},{80,96},{96,112},{1... | collective-permute-start | bytes 6152 | tf_op jit(solution)/shard_map/while/body/eval_jaxpr/ppermute | solution.py:27
  353.6 101.0 %all-gather.3.cloned.1.call-done = bf16[1024,1024]{1,0:T(8,128)(2,1)} async-done(((bf16[64,1024]{1,0:T(8,128)(2,1)}), bf16[1024,1024]{1,0:T(8,128)(2,1)}) %all-gather.3.cloned.1.call-update) | async-done | bytes 2097168 | tf_op jit(solution)/shard_map/all_gather | solution.py:143
  454.7 5.2 convolution_convert_fusion
  460.8 82.9 %reduce-scatter.2.cloned.1.call-done = bf16[64,1024]{1,0:T(8,128)(2,1)} async-done(((bf16[1024,1024]{1,0:T(8,128)(2,1)}), bf16[64,1024]{1,0:T(8,128)(2,1)}) %reduce-scatter.2.cloned.1.call-update) | async-done | bytes 131088 | tf_op jit(solution)/shard_map/reduce_scatter | solution.py:144
  (447 shorter events, 182.3 us)
Async XLA Ops:
  7.2 447.5 %all-gather.3.cloned.1.call-start = ((), (), s32[]{:S(2)}) async-start(), calls=%async_computation.1 | async-start | bytes 2228224 | tf_op jit(solution)/shard_map/all_gather | solution.py:143
  106.2 9.4 %collective-permute-start.1 = (f32[64,1,8,128]{3,0,2,1:T(8,128)S(1)}, f32[64,1,8,128]{3,0,2,1:T(8,128)}, u32[]{:S(2)}, u32[]{:S(2)}) collective-permute-start(f32[64,1,8,128]{3,0,2,1:T(8,128)S(1)} %get-tuple-element.342), channel_id=1, source_target_pairs={{240,0},{0,16},{16,32},{32,48},{48,64},{64,80},{80,96},{96,112},{1... | collective-permute-start | bytes 786440 | tf_op jit(solution)/shard_map/while/body/eval_jaxpr/ppermute | solution.py:27
  119.8 9.7 %collective-permute-start.1 = (f32[64,1,8,128]{3,0,2,1:T(8,128)S(1)}, f32[64,1,8,128]{3,0,2,1:T(8,128)}, u32[]{:S(2)}, u32[]{:S(2)}) collective-permute-start(f32[64,1,8,128]{3,0,2,1:T(8,128)S(1)} %get-tuple-element.342), channel_id=1, source_target_pairs={{240,0},{0,16},{16,32},{32,48},{48,64},{64,80},{80,96},{96,112},{1... | collective-permute-start | bytes 786440 | tf_op jit(solution)/shard_map/while/body/eval_jaxpr/ppermute | solution.py:27
  119.9 10.6 %collective-permute-start = (bf16[64,1,8,128]{3,0,2,1:T(8,128)(2,1)S(1)}, bf16[64,1,8,128]{3,0,2,1:T(8,128)(2,1)}, u32[]{:S(2)}, u32[]{:S(2)}) collective-permute-start(bf16[64,1,8,128]{3,0,2,1:T(8,128)(2,1)S(1)} %get-tuple-element.467), channel_id=1, source_target_pairs={{240,0},{0,16},{16,32},{32,48},{48,64},{64,80},{80,96},{96,112},{1... | collective-permute-start | bytes 393224 | tf_op jit(solution)/shard_map/while/body/eval_jaxpr/ppermute | solution.py:27
  133.9 9.8 %collective-permute-start = (bf16[64,1,8,128]{3,0,2,1:T(8,128)(2,1)S(1)}, bf16[64,1,8,128]{3,0,2,1:T(8,128)(2,1)}, u32[]{:S(2)}, u32[]{:S(2)}) collective-permute-start(bf16[64,1,8,128]{3,0,2,1:T(8,128)(2,1)S(1)} %get-tuple-element.467), channel_id=1, source_target_pairs={{240,0},{0,16},{16,32},{32,48},{48,64},{64,80},{80,96},{96,112},{1... | collective-permute-start | bytes 393224 | tf_op jit(solution)/shard_map/while/body/eval_jaxpr/ppermute | solution.py:27
  147.0 10.8 %collective-permute-start.1 = (f32[64,1,8,128]{3,0,2,1:T(8,128)S(1)}, f32[64,1,8,128]{3,0,2,1:T(8,128)}, u32[]{:S(2)}, u32[]{:S(2)}) collective-permute-start(f32[64,1,8,128]{3,0,2,1:T(8,128)S(1)} %get-tuple-element.342), channel_id=1, source_target_pairs={{240,0},{0,16},{16,32},{32,48},{48,64},{64,80},{80,96},{96,112},{1... | collective-permute-start | bytes 786440 | tf_op jit(solution)/shard_map/while/body/eval_jaxpr/ppermute | solution.py:27
  148.3 10.5 %collective-permute-start = (bf16[64,1,8,128]{3,0,2,1:T(8,128)(2,1)S(1)}, bf16[64,1,8,128]{3,0,2,1:T(8,128)(2,1)}, u32[]{:S(2)}, u32[]{:S(2)}) collective-permute-start(bf16[64,1,8,128]{3,0,2,1:T(8,128)(2,1)S(1)} %get-tuple-element.467), channel_id=1, source_target_pairs={{240,0},{0,16},{16,32},{32,48},{48,64},{64,80},{80,96},{96,112},{1... | collective-permute-start | bytes 393224 | tf_op jit(solution)/shard_map/while/body/eval_jaxpr/ppermute | solution.py:27
  162.1 11.0 %collective-permute-start.1 = (f32[64,1,8,128]{3,0,2,1:T(8,128)S(1)}, f32[64,1,8,128]{3,0,2,1:T(8,128)}, u32[]{:S(2)}, u32[]{:S(2)}) collective-permute-start(f32[64,1,8,128]{3,0,2,1:T(8,128)S(1)} %get-tuple-element.342), channel_id=1, source_target_pairs={{240,0},{0,16},{16,32},{32,48},{48,64},{64,80},{80,96},{96,112},{1... | collective-permute-start | bytes 786440 | tf_op jit(solution)/shard_map/while/body/eval_jaxpr/ppermute | solution.py:27
  164.3 9.7 %collective-permute-start = (bf16[64,1,8,128]{3,0,2,1:T(8,128)(2,1)S(1)}, bf16[64,1,8,128]{3,0,2,1:T(8,128)(2,1)}, u32[]{:S(2)}, u32[]{:S(2)}) collective-permute-start(bf16[64,1,8,128]{3,0,2,1:T(8,128)(2,1)S(1)} %get-tuple-element.467), channel_id=1, source_target_pairs={{240,0},{0,16},{16,32},{32,48},{48,64},{64,80},{80,96},{96,112},{1... | collective-permute-start | bytes 393224 | tf_op jit(solution)/shard_map/while/body/eval_jaxpr/ppermute | solution.py:27
  177.4 10.5 %collective-permute-start.1 = (f32[64,1,8,128]{3,0,2,1:T(8,128)S(1)}, f32[64,1,8,128]{3,0,2,1:T(8,128)}, u32[]{:S(2)}, u32[]{:S(2)}) collective-permute-start(f32[64,1,8,128]{3,0,2,1:T(8,128)S(1)} %get-tuple-element.342), channel_id=1, source_target_pairs={{240,0},{0,16},{16,32},{32,48},{48,64},{64,80},{80,96},{96,112},{1... | collective-permute-start | bytes 786440 | tf_op jit(solution)/shard_map/while/body/eval_jaxpr/ppermute | solution.py:27
  179.7 9.1 %collective-permute-start = (bf16[64,1,8,128]{3,0,2,1:T(8,128)(2,1)S(1)}, bf16[64,1,8,128]{3,0,2,1:T(8,128)(2,1)}, u32[]{:S(2)}, u32[]{:S(2)}) collective-permute-start(bf16[64,1,8,128]{3,0,2,1:T(8,128)(2,1)S(1)} %get-tuple-element.467), channel_id=1, source_target_pairs={{240,0},{0,16},{16,32},{32,48},{48,64},{64,80},{80,96},{96,112},{1... | collective-permute-start | bytes 393224 | tf_op jit(solution)/shard_map/while/body/eval_jaxpr/ppermute | solution.py:27
  192.1 10.5 %collective-permute-start.1 = (f32[64,1,8,128]{3,0,2,1:T(8,128)S(1)}, f32[64,1,8,128]{3,0,2,1:T(8,128)}, u32[]{:S(2)}, u32[]{:S(2)}) collective-permute-start(f32[64,1,8,128]{3,0,2,1:T(8,128)S(1)} %get-tuple-element.342), channel_id=1, source_target_pairs={{240,0},{0,16},{16,32},{32,48},{48,64},{64,80},{80,96},{96,112},{1... | collective-permute-start | bytes 786440 | tf_op jit(solution)/shard_map/while/body/eval_jaxpr/ppermute | solution.py:27
  194.3 9.2 %collective-permute-start = (bf16[64,1,8,128]{3,0,2,1:T(8,128)(2,1)S(1)}, bf16[64,1,8,128]{3,0,2,1:T(8,128)(2,1)}, u32[]{:S(2)}, u32[]{:S(2)}) collective-permute-start(bf16[64,1,8,128]{3,0,2,1:T(8,128)(2,1)S(1)} %get-tuple-element.467), channel_id=1, source_target_pairs={{240,0},{0,16},{16,32},{32,48},{48,64},{64,80},{80,96},{96,112},{1... | collective-permute-start | bytes 393224 | tf_op jit(solution)/shard_map/while/body/eval_jaxpr/ppermute | solution.py:27
  206.8 10.5 %collective-permute-start.1 = (f32[64,1,8,128]{3,0,2,1:T(8,128)S(1)}, f32[64,1,8,128]{3,0,2,1:T(8,128)}, u32[]{:S(2)}, u32[]{:S(2)}) collective-permute-start(f32[64,1,8,128]{3,0,2,1:T(8,128)S(1)} %get-tuple-element.342), channel_id=1, source_target_pairs={{240,0},{0,16},{16,32},{32,48},{48,64},{64,80},{80,96},{96,112},{1... | collective-permute-start | bytes 786440 | tf_op jit(solution)/shard_map/while/body/eval_jaxpr/ppermute | solution.py:27
  208.6 9.6 %collective-permute-start = (bf16[64,1,8,128]{3,0,2,1:T(8,128)(2,1)S(1)}, bf16[64,1,8,128]{3,0,2,1:T(8,128)(2,1)}, u32[]{:S(2)}, u32[]{:S(2)}) collective-permute-start(bf16[64,1,8,128]{3,0,2,1:T(8,128)(2,1)S(1)} %get-tuple-element.467), channel_id=1, source_target_pairs={{240,0},{0,16},{16,32},{32,48},{48,64},{64,80},{80,96},{96,112},{1... | collective-permute-start | bytes 393224 | tf_op jit(solution)/shard_map/while/body/eval_jaxpr/ppermute | solution.py:27
  221.6 10.5 %collective-permute-start.1 = (f32[64,1,8,128]{3,0,2,1:T(8,128)S(1)}, f32[64,1,8,128]{3,0,2,1:T(8,128)}, u32[]{:S(2)}, u32[]{:S(2)}) collective-permute-start(f32[64,1,8,128]{3,0,2,1:T(8,128)S(1)} %get-tuple-element.342), channel_id=1, source_target_pairs={{240,0},{0,16},{16,32},{32,48},{48,64},{64,80},{80,96},{96,112},{1... | collective-permute-start | bytes 786440 | tf_op jit(solution)/shard_map/while/body/eval_jaxpr/ppermute | solution.py:27
  223.3 9.6 %collective-permute-start = (bf16[64,1,8,128]{3,0,2,1:T(8,128)(2,1)S(1)}, bf16[64,1,8,128]{3,0,2,1:T(8,128)(2,1)}, u32[]{:S(2)}, u32[]{:S(2)}) collective-permute-start(bf16[64,1,8,128]{3,0,2,1:T(8,128)(2,1)S(1)} %get-tuple-element.467), channel_id=1, source_target_pairs={{240,0},{0,16},{16,32},{32,48},{48,64},{64,80},{80,96},{96,112},{1... | collective-permute-start | bytes 393224 | tf_op jit(solution)/shard_map/while/body/eval_jaxpr/ppermute | solution.py:27
  236.3 10.5 %collective-permute-start.1 = (f32[64,1,8,128]{3,0,2,1:T(8,128)S(1)}, f32[64,1,8,128]{3,0,2,1:T(8,128)}, u32[]{:S(2)}, u32[]{:S(2)}) collective-permute-start(f32[64,1,8,128]{3,0,2,1:T(8,128)S(1)} %get-tuple-element.342), channel_id=1, source_target_pairs={{240,0},{0,16},{16,32},{32,48},{48,64},{64,80},{80,96},{96,112},{1... | collective-permute-start | bytes 786440 | tf_op jit(solution)/shard_map/while/body/eval_jaxpr/ppermute | solution.py:27
  238.1 9.6 %collective-permute-start = (bf16[64,1,8,128]{3,0,2,1:T(8,128)(2,1)S(1)}, bf16[64,1,8,128]{3,0,2,1:T(8,128)(2,1)}, u32[]{:S(2)}, u32[]{:S(2)}) collective-permute-start(bf16[64,1,8,128]{3,0,2,1:T(8,128)(2,1)S(1)} %get-tuple-element.467), channel_id=1, source_target_pairs={{240,0},{0,16},{16,32},{32,48},{48,64},{64,80},{80,96},{96,112},{1... | collective-permute-start | bytes 393224 | tf_op jit(solution)/shard_map/while/body/eval_jaxpr/ppermute | solution.py:27
  251.0 10.5 %collective-permute-start.1 = (f32[64,1,8,128]{3,0,2,1:T(8,128)S(1)}, f32[64,1,8,128]{3,0,2,1:T(8,128)}, u32[]{:S(2)}, u32[]{:S(2)}) collective-permute-start(f32[64,1,8,128]{3,0,2,1:T(8,128)S(1)} %get-tuple-element.342), channel_id=1, source_target_pairs={{240,0},{0,16},{16,32},{32,48},{48,64},{64,80},{80,96},{96,112},{1... | collective-permute-start | bytes 786440 | tf_op jit(solution)/shard_map/while/body/eval_jaxpr/ppermute | solution.py:27
  252.8 9.6 %collective-permute-start = (bf16[64,1,8,128]{3,0,2,1:T(8,128)(2,1)S(1)}, bf16[64,1,8,128]{3,0,2,1:T(8,128)(2,1)}, u32[]{:S(2)}, u32[]{:S(2)}) collective-permute-start(bf16[64,1,8,128]{3,0,2,1:T(8,128)(2,1)S(1)} %get-tuple-element.467), channel_id=1, source_target_pairs={{240,0},{0,16},{16,32},{32,48},{48,64},{64,80},{80,96},{96,112},{1... | collective-permute-start | bytes 393224 | tf_op jit(solution)/shard_map/while/body/eval_jaxpr/ppermute | solution.py:27
  265.7 10.8 %collective-permute-start.1 = (f32[64,1,8,128]{3,0,2,1:T(8,128)S(1)}, f32[64,1,8,128]{3,0,2,1:T(8,128)}, u32[]{:S(2)}, u32[]{:S(2)}) collective-permute-start(f32[64,1,8,128]{3,0,2,1:T(8,128)S(1)} %get-tuple-element.342), channel_id=1, source_target_pairs={{240,0},{0,16},{16,32},{32,48},{48,64},{64,80},{80,96},{96,112},{1... | collective-permute-start | bytes 786440 | tf_op jit(solution)/shard_map/while/body/eval_jaxpr/ppermute | solution.py:27
  267.5 10.0 %collective-permute-start = (bf16[64,1,8,128]{3,0,2,1:T(8,128)(2,1)S(1)}, bf16[64,1,8,128]{3,0,2,1:T(8,128)(2,1)}, u32[]{:S(2)}, u32[]{:S(2)}) collective-permute-start(bf16[64,1,8,128]{3,0,2,1:T(8,128)(2,1)S(1)} %get-tuple-element.467), channel_id=1, source_target_pairs={{240,0},{0,16},{16,32},{32,48},{48,64},{64,80},{80,96},{96,112},{1... | collective-permute-start | bytes 393224 | tf_op jit(solution)/shard_map/while/body/eval_jaxpr/ppermute | solution.py:27
  280.8 11.9 %collective-permute-start.1 = (f32[64,1,8,128]{3,0,2,1:T(8,128)S(1)}, f32[64,1,8,128]{3,0,2,1:T(8,128)}, u32[]{:S(2)}, u32[]{:S(2)}) collective-permute-start(f32[64,1,8,128]{3,0,2,1:T(8,128)S(1)} %get-tuple-element.342), channel_id=1, source_target_pairs={{240,0},{0,16},{16,32},{32,48},{48,64},{64,80},{80,96},{96,112},{1... | collective-permute-start | bytes 786440 | tf_op jit(solution)/shard_map/while/body/eval_jaxpr/ppermute | solution.py:27
  282.5 11.2 %collective-permute-start = (bf16[64,1,8,128]{3,0,2,1:T(8,128)(2,1)S(1)}, bf16[64,1,8,128]{3,0,2,1:T(8,128)(2,1)}, u32[]{:S(2)}, u32[]{:S(2)}) collective-permute-start(bf16[64,1,8,128]{3,0,2,1:T(8,128)(2,1)S(1)} %get-tuple-element.467), channel_id=1, source_target_pairs={{240,0},{0,16},{16,32},{32,48},{48,64},{64,80},{80,96},{96,112},{1... | collective-permute-start | bytes 393224 | tf_op jit(solution)/shard_map/while/body/eval_jaxpr/ppermute | solution.py:27
  297.0 13.0 %collective-permute-start.1 = (f32[64,1,8,128]{3,0,2,1:T(8,128)S(1)}, f32[64,1,8,128]{3,0,2,1:T(8,128)}, u32[]{:S(2)}, u32[]{:S(2)}) collective-permute-start(f32[64,1,8,128]{3,0,2,1:T(8,128)S(1)} %get-tuple-element.342), channel_id=1, source_target_pairs={{240,0},{0,16},{16,32},{32,48},{48,64},{64,80},{80,96},{96,112},{1... | collective-permute-start | bytes 786440 | tf_op jit(solution)/shard_map/while/body/eval_jaxpr/ppermute | solution.py:27
  298.4 12.5 %collective-permute-start = (bf16[64,1,8,128]{3,0,2,1:T(8,128)(2,1)S(1)}, bf16[64,1,8,128]{3,0,2,1:T(8,128)(2,1)}, u32[]{:S(2)}, u32[]{:S(2)}) collective-permute-start(bf16[64,1,8,128]{3,0,2,1:T(8,128)(2,1)S(1)} %get-tuple-element.467), channel_id=1, source_target_pairs={{240,0},{0,16},{16,32},{32,48},{48,64},{64,80},{80,96},{96,112},{1... | collective-permute-start | bytes 393224 | tf_op jit(solution)/shard_map/while/body/eval_jaxpr/ppermute | solution.py:27
  314.2 13.3 %collective-permute-start.1 = (f32[64,1,8,128]{3,0,2,1:T(8,128)S(1)}, f32[64,1,8,128]{3,0,2,1:T(8,128)}, u32[]{:S(2)}, u32[]{:S(2)}) collective-permute-start(f32[64,1,8,128]{3,0,2,1:T(8,128)S(1)} %get-tuple-element.342), channel_id=1, source_target_pairs={{240,0},{0,16},{16,32},{32,48},{48,64},{64,80},{80,96},{96,112},{1... | collective-permute-start | bytes 786440 | tf_op jit(solution)/shard_map/while/body/eval_jaxpr/ppermute | solution.py:27
  315.7 12.8 %collective-permute-start = (bf16[64,1,8,128]{3,0,2,1:T(8,128)(2,1)S(1)}, bf16[64,1,8,128]{3,0,2,1:T(8,128)(2,1)}, u32[]{:S(2)}, u32[]{:S(2)}) collective-permute-start(bf16[64,1,8,128]{3,0,2,1:T(8,128)(2,1)S(1)} %get-tuple-element.467), channel_id=1, source_target_pairs={{240,0},{0,16},{16,32},{32,48},{48,64},{64,80},{80,96},{96,112},{1... | collective-permute-start | bytes 393224 | tf_op jit(solution)/shard_map/while/body/eval_jaxpr/ppermute | solution.py:27
  331.8 14.9 %collective-permute-start.1 = (f32[64,1,8,128]{3,0,2,1:T(8,128)S(1)}, f32[64,1,8,128]{3,0,2,1:T(8,128)}, u32[]{:S(2)}, u32[]{:S(2)}) collective-permute-start(f32[64,1,8,128]{3,0,2,1:T(8,128)S(1)} %get-tuple-element.342), channel_id=1, source_target_pairs={{240,0},{0,16},{16,32},{32,48},{48,64},{64,80},{80,96},{96,112},{1... | collective-permute-start | bytes 786440 | tf_op jit(solution)/shard_map/while/body/eval_jaxpr/ppermute | solution.py:27
  333.6 14.1 %collective-permute-start = (bf16[64,1,8,128]{3,0,2,1:T(8,128)(2,1)S(1)}, bf16[64,1,8,128]{3,0,2,1:T(8,128)(2,1)}, u32[]{:S(2)}, u32[]{:S(2)}) collective-permute-start(bf16[64,1,8,128]{3,0,2,1:T(8,128)(2,1)S(1)} %get-tuple-element.467), channel_id=1, source_target_pairs={{240,0},{0,16},{16,32},{32,48},{48,64},{64,80},{80,96},{96,112},{1... | collective-permute-start | bytes 393224 | tf_op jit(solution)/shard_map/while/body/eval_jaxpr/ppermute | solution.py:27
  353.6 190.1 %reduce-scatter.2.cloned.1.call-start = ((), (), s32[]{:S(2)}) async-start(), calls=%async_computation.2 | async-start | bytes 2228224 | tf_op jit(solution)/shard_map/reduce_scatter | solution.py:144
  (40 other events, 751.6 us)
Sparse Core Ops, SparseCore 0:
  353.7 100.9 all-gather.2
  460.0 83.5 reduce-scatter.1
where the time goes:
time: 553 us; the launch traced here: 551 us
  waiting for transfers between devices  209 us (38%)
  starting transfers between devices  152 us (27%)
  blocking collectives  85.2 us (15%)
  local copies, waits for them, and re-layouts  37 us (7%)
  matrix products  34 us (6%)
  other arithmetic  16.7 us (3%)
  between operations  15.6 us (3%)
    ppermute x64, starting transfers between devices, from_behind(): return lax.ppermute(block, axis, route)  152 us
    all_gather x1, waiting for transfers between devices, local(): every_row = lax.all_gather(flat_rows, 'ctx', axis=0, tiled=True)  101 us
    reduce_scatter x1, waiting for transfers between devices, local(): lax.psum_scatter(jnp.dot(every_row, out_weight, preferred_element_type=jn...  82.9 us
    all_gather x1, blocking collectives, local(): lax.all_gather(span_vals, 'ctx', axis=1, tiled=True)  44.7 us
    ppermute x64, waiting for transfers between devices, from_behind(): return lax.ppermute(block, axis, route)  24.8 us
    all_gather x1, blocking collectives, local(): lax.all_gather(span_here, 'ctx', axis=1, tiled=True)  23.9 us
    unnamed x1, blocking collectives  16.6 us
    while x80, local copies, waits for them, and re-layouts  15.4 us
  transfers between devices with their start and end apart: 66, of which 21 were waited for; matrix products, arithmetic and copies ran while one was open for 3% of the time, Pallas kernels for 0%

commit v1 on v0

v1 whole, which is shorter than its diff:
```python
import functools
import math

import jax
import jax.numpy as jnp
from jax import lax
from jax.experimental import pallas as pl
from jax.experimental.pallas import tpu as pltpu
from jax.sharding import Mesh, PartitionSpec as P

H = 128
KVH = 8
HD = 128
NEG = -1e30
C2 = math.log2(math.e) / math.sqrt(HD)
TILE = 512
ROWS = 512
STAT = 32
NZ = 8
SAFE = 90.0
F32 = jnp.float32
BF16 = jnp.bfloat16
MB = 1024 * 1024


def eye_mask():
    r = lax.broadcasted_iota(jnp.int32, (128, 128), 0)
    c = lax.broadcasted_iota(jnp.int32, (128, 128), 1)
    return r == c


def split3(x):
    hi = x.astype(BF16)
    rest = x - hi.astype(F32)
    mid = rest.astype(BF16)
    lo = (rest - mid.astype(F32)).astype(BF16)
    return hi, mid, lo


def pack_kernel(place, ck, cv, sk, sv, near_out, far_out, rest_out, sem):
    core, kv = place[0], place[2]
    n = ck.shape[1]

    def copies(cache, span, out, head, first):
        return [
            pltpu.make_async_copy(cache.at[head], out.at[pl.ds(0, n)], sem.at[first]),
            pltpu.make_async_copy(span.at[head], out.at[pl.ds(n, 64)], sem.at[first + 1]),
        ]

    def move(cache, span, cache2, span2):
        mine = copies(cache, span, far_out, kv ^ 1, 0) + copies(cache, span, near_out, kv, 2)
        mine += copies(cache2, span2, rest_out, kv, 4)
        for c in mine:
            c.start()
        for c in mine:
            c.wait()

    pl.when(core == 0)(lambda: move(ck, sk, cv, sv))
    pl.when(core == 1)(lambda: move(cv, sv, ck, sk))


def pack(place, ck, cv, sk, sv):
    n = ck.shape[1] + 64
    shape = jax.ShapeDtypeStruct((n, HD), BF16)
    return pl.pallas_call(
        pack_kernel,
        out_shape=[shape] * 3,
        in_specs=[pl.BlockSpec(memory_space=pltpu.SMEM)] + [pl.BlockSpec(memory_space=pl.ANY)] * 4,
        out_specs=[pl.BlockSpec(memory_space=pltpu.VMEM)] * 3,
        scratch_shapes=[pltpu.SemaphoreType.DMA((6,))],
        compiler_params=pltpu.CompilerParams(vmem_limit_bytes=57 * MB),
        name="pack",
    )(place, ck, cv, sk, sv)


def payload_kernel(own, x, z, zx, q_ref, out_ref):
    lens = [own[0], x[0], z[0], zx[0]]
    out_ref[0:ROWS, :] = q_ref[...]
    q = q_ref[...].astype(F32)
    norm = jnp.max(jnp.sum(q * q, axis=-1, keepdims=True), axis=0, keepdims=True)
    lane = lax.broadcasted_iota(jnp.int32, (16, 128), 1)
    row = jnp.where(lane == 8, norm * 1.02, 0.0)
    for i in range(4):
        row = jnp.where(lane == 2 * i, (lens[i] // 64).astype(F32), row)
        row = jnp.where(lane == 2 * i + 1, (lens[i] % 64).astype(F32), row)
    out_ref[ROWS:ROWS + 16, :] = row.astype(BF16)


def payload(lengths, q):
    smem, vmem = pl.BlockSpec(memory_space=pltpu.SMEM), pl.BlockSpec(memory_space=pltpu.VMEM)
    return pl.pallas_call(
        payload_kernel,
        out_shape=jax.ShapeDtypeStruct((ROWS + 16, HD), BF16),
        in_specs=[smem] * 4 + [vmem],
        out_specs=vmem,
        compiler_params=pltpu.CompilerParams(vmem_limit_bytes=8 * MB),
        name="payload",
    )(*lengths, q)


def assemble_kernel(place, start, *refs):
    qs, bufs, (k_all, v_all, meta, sem) = refs[:4], refs[4:12], refs[12:]
    core, xl, z = place[0], place[1], place[3]
    sign = 1 - 2 * core
    firsts, seconds = bufs[0::2], bufs[1::2]

    def copies(keys, vals):
        pairs = [(k, k_all.at[i]) for i, k in enumerate(keys)] + [(v, v_all.at[i]) for i, v in enumerate(vals)]
        return [pltpu.make_async_copy(s, d, sem.at[i]) for i, (s, d) in enumerate(pairs)]

    def move(keys, vals):
        mine = copies(keys, vals)
        for c in mine:
            c.start()
        for c in mine:
            c.wait()

    pl.when(core == 0)(lambda: move(firsts, seconds))
    pl.when(core == 1)(lambda: move(seconds, firsts))

    lane = lax.broadcasted_iota(jnp.int32, (1, 128), 1)
    rows = [q[ROWS:ROWS + 16, :].astype(F32)[0:1, :] for q in qs]
    pick = lambda i: jnp.where(lane == 2 * i, 64.0, jnp.where(lane == 2 * i + 1, 1.0, 0.0))
    odd = lax.rem(z, 2)
    size = [jnp.sum(rows[0] * pick(i)) for i in range(4)]
    total = functools.reduce(jnp.add, rows)
    before = jnp.zeros((1, 128), F32)
    for j, row in enumerate(rows):
        at = lax.rem(z - 2 * sign * j + 2 * NZ, NZ)
        before += jnp.where(at < z, row, 0.0)
    sums = [jnp.sum(before * pick(i)) for i in range(4)]
    alls = [jnp.sum(total * pick(i)) for i in range(4)]
    low = jnp.where(xl == 0, alls[0] + alls[2], alls[1] + alls[3])
    for i in range(4):
        side, other = i % 2, i // 2
        pairs_before = sums[side] + sums[2 + side]
        own_odd = odd if other == 0 else 1 - odd
        mate = size[(2 - 2 * other) + side]
        offset = pairs_before + jnp.where(own_odd == 1, mate, 0.0)
        upper = xl if side == 0 else 1 - xl
        offset += jnp.where(upper == 1, low, 0.0)
        live = jnp.clip(start[0] - offset.astype(jnp.int32), 0, size[i].astype(jnp.int32))
        meta[i] = live
        zz = z if other == 0 else z + 1 - 2 * odd
        meta[4 + i] = (upper * NZ + zz) * 64
    meta[8] = z
    meta[9] = xl * 512
    meta[10] = sign
    q2 = jnp.sum(jnp.where(lane == 8, functools.reduce(jnp.maximum, rows), 0.0))
    ones = jnp.ones((8, HD), BF16)
    k2 = jnp.zeros((8, 1), F32)
    for i in range(4):
        k = k_all[i]
        norms = lax.dot_general(ones, k * k, (((1,), (1,)), ((), ())), preferred_element_type=F32)
        k2 = jnp.maximum(k2, jnp.max(norms, axis=-1, keepdims=True))
    meta[11] = jnp.where(q2 * jnp.max(k2) * 1.04 <= (SAFE / C2) ** 2, 1, 0).astype(jnp.int32)


def assemble(place, start, qs, bufs):
    smem, vmem = pl.BlockSpec(memory_space=pltpu.SMEM), pl.BlockSpec(memory_space=pltpu.VMEM)
    everything = jax.ShapeDtypeStruct((4,) + bufs[0].shape, BF16)
    return pl.pallas_call(
        assemble_kernel,
        out_shape=[everything, everything, jax.ShapeDtypeStruct((12,), jnp.int32)],
        in_specs=[smem, smem] + [vmem] * 4 + [pl.BlockSpec(memory_space=pl.ANY)] * 8,
        out_specs=[vmem, vmem, smem],
        scratch_shapes=[pltpu.SemaphoreType.DMA((8,))],
        compiler_params=pltpu.CompilerParams(vmem_limit_bytes=24 * MB),
        name="assemble",
    )(place, start, *qs, *bufs)


def unpack_stats(st):
    g = ROWS // 128
    return st[0:g] + st[g:2 * g] + st[2 * g:3 * g], st[3 * g:4 * g] + st[4 * g:5 * g] + st[5 * g:6 * g]


def columns(rows):
    rows = jnp.concatenate([rows, jnp.zeros((128 - rows.shape[0], 128), F32)], axis=0)
    return jnp.transpose(rows)


def attend_kernel(hop, carried, meta, *refs):
    refs = list(refs)
    take = lambda n: [refs.pop(0) for _ in range(n)]
    q_ref, k_all, v_all = take(3)
    came = take(1)[0] if carried else None
    out_ref, meta_out = take(2)
    s_ref, span_ref, m_ref, acc_ref, total_ref = refs
    for i in range(12):
        meta_out[i] = meta[i]
    z, base, sign, small = (meta[i] for i in range(8, 12))
    cache = k_all.shape[1] - 64
    ones = jnp.ones((1024, 128), BF16)
    eye = eye_mask()
    g = ROWS // 128
    token0 = base + lax.rem(z - 2 * sign * hop + 2 * NZ, NZ) * 64

    def scores_of(keys):
        return lax.dot_general(q_ref[0:ROWS, :], keys, (((1,), (1,)), ((), ())), preferred_element_type=F32)

    def span_scores():
        s = scores_of(jnp.concatenate([k_all[i, pl.ds(cache, 64), :] for i in range(4)], axis=0))
        col = lax.broadcasted_iota(jnp.int32, (1, 256), 1)
        owner = col // 64
        pos = col % 64
        for i in range(4):
            pos = jnp.where(owner == i, pos + meta[4 + i], pos)
        row = lax.broadcasted_iota(jnp.int32, s.shape, 0)
        return jnp.where(pos <= token0 + row // 8, s, NEG)

    def span_sums(p):
        values = jnp.concatenate([v_all[i, pl.ds(cache, 64), :] for i in range(4)], axis=0)
        return jnp.dot(p, jnp.concatenate([values, ones[:256]], axis=1), preferred_element_type=F32)

    @pl.when(small == 1)
    def _():
        acc_ref[...] = span_sums(jnp.exp2(span_scores() * C2).astype(BF16))

        def shard(i, carry):
            live = meta[i]

            def piece(first, size):
                at = pl.ds(pl.multiple_of(first, 256), size)
                slot = first + lax.broadcasted_iota(jnp.int32, (1, size), 1)
                bias = jnp.where(slot < live, 0.0, NEG)
                p = jnp.exp2(scores_of(k_all[i, at, :]) * C2 + bias).astype(BF16)
                v = jnp.concatenate([v_all[i, at, :], ones[:size]], axis=1)
                acc_ref[...] += jnp.dot(p, v, preferred_element_type=F32)

            def body(t, carry):
                piece(t * 1024, 1024)
                return carry

            n = (live + 255) // 256
            whole = n // 4
            lax.fori_loop(0, whole, body, 0)
            pl.when(n % 4 >= 2)(lambda: piece(whole * 1024, 512))
            pl.when(n % 2 == 1)(lambda: piece((n - 1) * 256, 256))
            return carry

        lax.fori_loop(0, 4, shard, 0)
        m_ref[...] = jnp.where(acc_ref[:, 128:256] > 0.0, 0.0, NEG)

    @pl.when(small == 0)
    def _():
        half = lambda x: functools.reduce(jnp.maximum, [x[:, j:j + 128] for j in range(0, x.shape[1], 128)])
        s = span_scores()
        span_ref[...] = s
        m_ref[...] = half(s)

        def score_shard(i, first):
            live = meta[i]
            tiles = (live + TILE - 1) // TILE

            def score(t, carry):
                at = pl.ds(pl.multiple_of(t * TILE, TILE), TILE)
                slot = t * TILE + lax.broadcasted_iota(jnp.int32, (1, TILE), 1)
                s = scores_of(k_all[i, at, :]) + jnp.where(slot < live, 0.0, NEG)
                s_ref[first + t] = s
                m_ref[...] = jnp.maximum(m_ref[...], half(s))
                return carry

            lax.fori_loop(0, tiles, score, 0)
            return first + tiles

        lax.fori_loop(0, 4, score_shard, jnp.int32(0))
        m = jnp.broadcast_to(jnp.max(m_ref[...], axis=-1, keepdims=True), (ROWS, 128))
        m_ref[...] = m
        s = span_ref[...]
        wide = jnp.concatenate([m, m], axis=1)
        acc_ref[...] = span_sums(jnp.where(s > 0.5 * NEG, jnp.exp2((s - wide) * C2), 0.0).astype(BF16))

        def value_shard(i, first):
            tiles = (meta[i] + TILE - 1) // TILE

            def value(t, carry):
                at = pl.ds(pl.multiple_of(t * TILE, TILE), TILE)
                wide = jnp.concatenate([m_ref[...]] * (TILE // 128), axis=1)
                p = jnp.exp2((s_ref[first + t] - wide) * C2).astype(BF16)
                v = jnp.concatenate([v_all[i, at, :], ones[:TILE]], axis=1)
                acc_ref[...] += jnp.dot(p, v, preferred_element_type=F32)
                return carry

            lax.fori_loop(0, tiles, value, 0)
            return first + tiles

        lax.fori_loop(0, 4, value_shard, jnp.int32(0))

    if carried:
        ms, ls = unpack_stats(came[ROWS:ROWS + STAT, :].astype(F32))
        ft = columns(jnp.concatenate([ms, ls], axis=0))
        for r in range(g):
            at = slice(r * 128, (r + 1) * 128)
            m_in = jnp.broadcast_to(ft[:, r:r + 1], (128, 128))
            l_in = jnp.broadcast_to(ft[:, g + r:g + r + 1], (128, 128))
            m_own = m_ref[at, :]
            m = jnp.maximum(m_own, m_in)
            w_own = jnp.exp2((m_own - m) * C2)
            w_in = jnp.exp2((m_in - m) * C2) * l_in
            total = acc_ref[at, 128:256] * w_own + w_in
            mixed = acc_ref[at, 0:128] * w_own + came[at, :].astype(F32) * w_in
            out_ref[at, :] = (mixed / jnp.maximum(total, 1e-35)).astype(BF16)
            m_ref[at, :] = m
            total_ref[at, :] = total
    else:
        total = acc_ref[:, 128:256]
        out_ref[0:ROWS, :] = (acc_ref[:, 0:128] / jnp.maximum(total, 1e-35)).astype(BF16)
        total_ref[...] = total

    compact = lambda x: jnp.sum(jnp.where(eye[None], x.reshape(g, 128, 128), 0.0), axis=1)
    stats = split3(compact(m_ref[...])) + split3(compact(total_ref[...]))
    pad = jnp.zeros((STAT - 6 * g, 128), F32)
    out_ref[ROWS:ROWS + STAT, :] = jnp.concatenate([x.astype(F32) for x in stats] + [pad], axis=0).astype(BF16)


def attend(hop, meta, q, k_all, v_all, came):
    smem, vmem = pl.BlockSpec(memory_space=pltpu.SMEM), pl.BlockSpec(memory_space=pltpu.VMEM)
    tiles = 4 * (k_all.shape[1] - 64) // TILE
    came = [] if came is None else [came]
    return pl.pallas_call(
        functools.partial(attend_kernel, hop, bool(came)),
        out_shape=[jax.ShapeDtypeStruct((ROWS + STAT, 128), BF16), jax.ShapeDtypeStruct((12,), jnp.int32)],
        in_specs=[smem] + [vmem] * (3 + len(came)),
        out_specs=[vmem, smem],
        scratch_shapes=[
            pltpu.VMEM((tiles, ROWS, TILE), F32),
            pltpu.VMEM((ROWS, 256), F32),
            pltpu.VMEM((ROWS, 128), F32),
            pltpu.VMEM((ROWS, 256), F32),
            pltpu.VMEM((ROWS, 128), F32),
        ],
        compiler_params=pltpu.CompilerParams(vmem_limit_bytes=28 * MB),
        cost_estimate=pl.CostEstimate(flops=600_000_000, bytes_accessed=100_000, transcendentals=1_000),
        name="attend",
    )(meta, q, k_all, v_all, *came)


def combine_kernel(place, *refs):
    parts, (out_ref, *piece_refs, f_ref, flat_ref) = refs[:-7], refs[-7:]
    g = ROWS // 128
    ms, ls = zip(*[unpack_stats(ref[ROWS:ROWS + STAT, :].astype(F32)) for ref in parts])
    top = functools.reduce(jnp.maximum, ms)
    ws = [jnp.exp2((m - top) * C2) * l for m, l in zip(ms, ls)]
    whole = functools.reduce(jnp.add, ws)
    ft = columns(jnp.concatenate([w / whole for w in ws], axis=0))
    for r in range(g):
        total = jnp.zeros((128, 128), F32)
        for k, ref in enumerate(parts):
            total += ref[r * 128:(r + 1) * 128, :].astype(F32) * ft[:, k * g + r:k * g + r + 1]
        out_ref[r * 128:(r + 1) * 128, :] = total.astype(BF16)
        f_ref[r * 128:(r + 1) * 128, :] = total
    for h in range(8):
        flat_ref[:, h * 128:(h + 1) * 128] = f_ref[pl.ds(h, 64, stride=8), :].astype(BF16)
    core, xl = place[0], place[1]
    for i, ref in enumerate(piece_refs):
        c = core if i % 2 == 0 else 1 - core
        x = xl if i // 2 == 0 else 1 - xl
        ref[...] = flat_ref[pl.ds(pl.multiple_of(x * 32 + c * 16, 16), 16), :]


def combine(place, parts):
    vmem = pl.BlockSpec(memory_space=pltpu.VMEM)
    piece = jax.ShapeDtypeStruct((16, 1024), BF16)
    return pl.pallas_call(
        combine_kernel,
        out_shape=[jax.ShapeDtypeStruct((ROWS, 128), BF16)] + [piece] * 4,
        in_specs=[pl.BlockSpec(memory_space=pltpu.SMEM)] + [vmem] * len(parts),
        out_specs=[vmem] * 5,
        scratch_shapes=[pltpu.VMEM((ROWS, 128), F32), pltpu.VMEM((64, 1024), BF16)],
        compiler_params=pltpu.CompilerParams(vmem_limit_bytes=16 * MB),
        name="combine",
    )(place, *parts)


def local(queries, cache_keys, cache_values, span_keys, span_values, span_start, cache_lengths, out_weight):
    xl, z, y, xh, core = (lax.axis_index(a) for a in ("xl", "z", "y", "xh", "core"))
    sign = 1 - 2 * core
    kv = y * 2 + xh
    place = jnp.stack([core, xl, kv, z]).astype(jnp.int32)

    def shift(x, k):
        pairs = [(b * 2 + c, (b + k * (1 - 2 * c)) % NZ * 2 + c) for b in range(NZ) for c in range(2)]
        return lax.ppermute(x, ("z", "core"), pairs)

    swap = [(0, 1), (1, 0)]
    cross = [(i, 3 - i) for i in range(4)]
    mate = [(i, i ^ 1) for i in range(NZ)]

    near, far, rest = pack(place, cache_keys, cache_values, span_keys, span_values)
    got_x = lax.ppermute(far, ("xl", "xh"), cross)
    got_z = lax.ppermute(near, "z", mate)

    both = [((a * NZ + b) * 2 + c, ((1 - a) * NZ + (b ^ 1)) * 2 + 1 - c) for a in range(2) for b in range(NZ) for c in range(2)]
    lengths = [
        cache_lengths,
        lax.ppermute(cache_lengths, ("xl", "xh"), cross),
        lax.ppermute(cache_lengths, "z", mate),
        lax.ppermute(cache_lengths, ("xl", "z", "xh"), both),
    ]
    q = payload(lengths, queries.reshape(ROWS, HD))
    q_blocks = [q, shift(q, 2), None, shift(q, -2)]
    q_blocks[2] = shift(q_blocks[1], 2)
    got_x, got_z, q_blocks[2], q_blocks[3], weight = lax.optimization_barrier(
        (got_x, got_z, q_blocks[2], q_blocks[3], out_weight)
    )
    got_zx = lax.ppermute(got_x, "z", mate)
    w_x = lax.ppermute(weight, "xl", swap)
    w_core = lax.ppermute(weight, "core", swap)
    bufs = [near, rest]
    for got in (got_x, got_z, got_zx):
        bufs += [got, lax.ppermute(got, "core", swap)]
    k_all, v_all, meta = assemble(place, span_start, q_blocks, bufs)

    out, meta = attend(2, meta, q_blocks[2], k_all, v_all, None)
    half_way = shift(out, 2)
    out, meta = attend(1, meta, q_blocks[1], k_all, v_all, None)
    down = shift(out, -2)
    out, meta = attend(3, meta, q_blocks[3], k_all, v_all, half_way)
    up = shift(out, 2)
    own, meta = attend(0, meta, q_blocks[0], k_all, v_all, None)
    own, w_x = lax.optimization_barrier((own, w_x))
    w_both = lax.ppermute(w_x, "core", swap)
    mixed, *pieces = combine(place, [own, up, down])
    attended = mixed.reshape(64, 8, HD)

    p_core = lax.ppermute(pieces[1], "core", swap)
    p_x = lax.ppermute(pieces[2], "xl", swap)
    p_both = lax.ppermute(pieces[3], ("xl", "core"), cross)
    here = jnp.concatenate([pieces[0], p_core], axis=1)
    there = jnp.concatenate([p_x, p_both], axis=1)
    pair = jnp.stack([jnp.where(xl == 0, here, there), jnp.where(xl == 0, there, here)])[:, None]
    every = jnp.zeros((2, NZ, 16, 2048), BF16)
    every = lax.dynamic_update_slice(every, pair, (0, z, 0, 0))
    up = down = pair
    for k in range(1, 5):
        up = shift(up, 1)
        every = lax.dynamic_update_slice(every, up, (0, (z - sign * k + 2 * NZ) % NZ, 0, 0))
        if k < 4:
            down = shift(down, -1)
            every = lax.dynamic_update_slice(every, down, (0, (z + sign * k + 2 * NZ) % NZ, 0, 0))
    x = every.reshape(256, 2048)

    def term(top, low):
        part = jnp.dot(x[:, 0:1024], top, preferred_element_type=F32)
        return (part + jnp.dot(x[:, 1024:2048], low, preferred_element_type=F32)).astype(BF16)

    t_own, t_peer = term(out_weight, w_core), term(w_x, w_both)
    terms = jnp.stack([jnp.where(xl == 0, t_own, t_peer), jnp.where(xl == 0, t_peer, t_own)])
    got = lax.all_to_all(terms.reshape(32, 16, 1024), ("xl", "y", "xh", "core"), 0, 0, tiled=True)
    projected = jnp.sum(got.reshape(2, 8, 2, 16, 1024).astype(F32), axis=1).astype(BF16).reshape(64, 1024)
    return attended, projected


def solution(mesh):
    fine = Mesh(mesh.devices.reshape(2, NZ, 4, 2, 2), ("xl", "z", "y", "xh", "core"))
    ctx, tp = ("xl", "z"), ("y", "xh", "core")
    return jax.shard_map(
        local,
        mesh=fine,
        in_specs=(
            P(ctx, tp, None),
            P(None, ctx, None),
            P(None, ctx, None),
            P(None, ctx, None),
            P(None, ctx, None),
            P(),
            P(ctx),
            P(tp, ctx),
        ),
        out_specs=(P(ctx, tp, None), P(tp, ctx)),
        check_vma=False,
    )
```

time: 553 us -> 157 us (0.28)
  waiting for transfers between devices: 209 us -> 31.1 us
  starting transfers between devices: 152 us -> 47.8 us
  blocking collectives: 85.2 us -> 31.9 us
  Pallas kernels: 0 us -> 38.8 us
  local copies, waits for them, and re-layouts: 37 us -> 3.18 us
  matrix products: 34 us -> 2.84 us
  other arithmetic: 16.7 us -> 1.56 us
  between operations: 15.6 us -> 2.28 us
    ppermute x64 -> x28, starting transfers between devices: 152 us -> 47.8 us  [the longest x13 22.6 us: shift(): return lax.ppermute(x, ('z', 'core'), pairs)]
    all_gather x1 -> x0, waiting for transfers between devices: 101 us -> none  [local(): every_row = lax.all_gather(flat_rows, 'ctx', axis=0, tiled=True)]
    reduce_scatter x1 -> x0, waiting for transfers between devices: 82.9 us -> none  [local(): lax.psum_scatter(jnp.dot(every_row, out_weight, preferred_element_type=jn...]
    all_gather x2 -> x0, blocking collectives: 68.7 us -> none  [the longest x1 44.7 us: local(): lax.all_gather(span_vals, 'ctx', axis=1, tiled=True)]
    pallas_call x0 -> x8, Pallas kernels: none -> 38.8 us  [the longest x4 29.3 us: attend(): pl.pallas_call(functools.partial(attend_kernel, hop, bool(came)), out_sha...]
    all_to_all x0 -> x1, blocking collectives: none -> 31.9 us  [local(): lax.all_to_all(terms.reshape(32, 16, 1024), ('xl', 'y', 'xh', 'core'), 0,...]
    dot_general x67 -> x4, matrix products: 34 us -> 2.84 us  [the longest x2 1.43 us: term(): part = jnp.dot(x[:, 0:1024], top, preferred_element_type=F32)]
    unnamed x1 -> x0, blocking collectives: 16.6 us -> none
  transfers between devices with their start and end apart: 66 -> 28, of which waited for: 21 -> 13; matrix products, arithmetic and copies ran while one was open for 3% -> 1% of each run, Pallas kernels for 0% -> 21%
where the time goes in v1:
time: 157 us; the launch traced here: 159 us
  starting transfers between devices  47.8 us (30%)
  Pallas kernels  38.8 us (25%)
  blocking collectives  31.9 us (20%)
  waiting for transfers between devices  31.1 us (20%)
  local copies, waits for them, and re-layouts  3.18 us (2%)
  matrix products  2.84 us (2%)
  between operations  2.28 us (1%)
    all_to_all x1, blocking collectives, local(): lax.all_to_all(terms.reshape(32, 16, 1024), ('xl', 'y', 'xh', 'core'), 0,...  31.9 us
    pallas_call x4, Pallas kernels, attend(): pl.pallas_call(functools.partial(attend_kernel, hop, bool(came)), out_sha...  29.3 us
    ppermute x13, starting transfers between devices, shift(): return lax.ppermute(x, ('z', 'core'), pairs)  22.6 us
    ppermute x13, waiting for transfers between devices, shift(): return lax.ppermute(x, ('z', 'core'), pairs)  17 us
    ppermute x3, starting transfers between devices, local(): bufs += [got, lax.ppermute(got, 'core', swap)]  10.5 us
    ppermute x1, waiting for transfers between devices, local(): lax.ppermute(cache_lengths, ('xl', 'xh'), cross)  7.23 us
    ppermute x1, waiting for transfers between devices, local(): got_zx = lax.ppermute(got_x, 'z', mate)  4.21 us
    ppermute x1, starting transfers between devices, local(): lax.ppermute(cache_lengths, ('xl', 'z', 'xh'), both)  3.56 us
  transfers between devices with their start and end apart: 28, of which 13 were waited for; matrix products, arithmetic and copies ran while one was open for 1% of the time, Pallas kernels for 21%

profile of v1, /device:TPU:1, one launch (start us, length us, event | category | flops | bytes accessed | tf_op | source)
XLA Modules:
  0.0 159.3 jit_solution(9452451712717728900)
XLA Ops:
  1.2 3.4 %pack.1 = (bf16[2112,128]{1,0:T(8,128)(2,1)}, bf16[2112,128]{1,0:T(8,128)(2,1)}, bf16[2112,128]{1,0:T(8,128)(2,1)}) custom-call(s32[4]{0:T(128)} %pad_add_fusion.place, bf16[8,2048,128]{2,1,0:T(8,128)(2,1)} %ck.1, bf16[8,2048,128]{2,1,0:T(8,128)(2,1)} %cv.1, bf16[8,64,128]{2,1,0:T(8,128)(2,1)} %sk.1, bf16[8,64,128]{2,1,0:T(8,128)(2,1)} %sv.1), custom_call_target="tpu_custom_call" | custom-call | tf_op jit(solution)/shard_map/pack/pallas_call | solution.py:65
  4.6 2.6 %collective-permute-start.5 = (bf16[2112,128]{1,0:T(8,128)(2,1)}, bf16[2112,128]{1,0:T(8,128)(2,1)S(1)}, u32[]{:S(2)}, u32[]{:S(2)}) collective-permute-start(bf16[2112,128]{1,0:T(8,128)(2,1)} %get-tuple-element.28.refs_4_), channel_id=1, source_target_pairs={{0,16},{16,0},{32,48},{48,32},{64,80},{80,64},{96,112},{112,96},{1... | collective-permute-start | bytes 1622024 | tf_op jit(solution)/shard_map/ppermute | solution.py:392
  7.2 2.5 %collective-permute-start.4 = (bf16[2112,128]{1,0:T(8,128)(2,1)}, bf16[2112,128]{1,0:T(8,128)(2,1)S(1)}, u32[]{:S(2)}, u32[]{:S(2)}) collective-permute-start(bf16[2112,128]{1,0:T(8,128)(2,1)} %get-tuple-element.27), channel_id=1, source_target_pairs={{0,130},{2,128},{128,2},{130,0},{1,131},{3,129},{129,3},{131,1},{4... | collective-permute-start | bytes 1622024 | tf_op jit(solution)/shard_map/ppermute | solution.py:391
  10.0 3.6 %collective-permute-start.2 = (s32[1]{0:T(128)}, s32[1]{0:T(128)}, u32[]{:S(2)}, u32[]{:S(2)}) collective-permute-start(s32[1]{0:T(128)} %param.14), channel_id=1, source_target_pairs={{0,146},{2,144},{16,130},{18,128},{32,178},{34,176},{48,162},{50,1... | collective-permute-start | bytes 20 | tf_op jit(solution)/shard_map/ppermute | solution.py:399
  14.2 7.2 %collective-permute-done.x = s32[1]{0:T(128)} collective-permute-done((s32[1]{0:T(128)}, s32[1]{0:T(128)}, u32[]{:S(2)}, u32[]{:S(2)}) %collective-permute-start) | collective-permute-done | bytes 36 | tf_op jit(solution)/shard_map/ppermute | solution.py:397
  21.5 1.9 %payload.1.refs_0_ = bf16[528,128]{1,0:T(8,128)(2,1)S(1)} custom-call(s32[1]{0:T(128)S(6)} %copy.27.own, s32[1]{0:T(128)} %collective-permute-done.x, s32[1]{0:T(128)} %collective-permute-done.1.z, s32[1]{0:T(128)} %collective-permute-done.2.zx, bf16[512,128]{1,0:T(8,128)(2,1)S(1)} %bitcast.41), custom_call_target="tpu_custom_call" | custom-call | tf_op jit(solution)/shard_map/payload/pallas_call | solution.py:91
  23.4 5.4 %collective-permute-start.3 = (bf16[528,128]{1,0:T(8,128)(2,1)S(1)}, bf16[528,128]{1,0:T(8,128)(2,1)S(1)}, u32[]{:S(2)}, u32[]{:S(2)}) collective-permute-start(bf16[528,128]{1,0:T(8,128)(2,1)S(1)} %payload.1.refs_0_), channel_id=1, source_target_pairs={{0,32},{1,97},{16,48},{17,113},{32,64},{33,1},{48,80},{49,17},{64,... | collective-permute-start | bytes 405512 | tf_op jit(solution)/shard_map/ppermute | solution.py:384
  28.8 3.6 %collective-permute-done.3.refs_1_.refs_0_ = bf16[528,128]{1,0:T(8,128)(2,1)S(1)} collective-permute-done((bf16[528,128]{1,0:T(8,128)(2,1)S(1)}, bf16[528,128]{1,0:T(8,128)(2,1)S(1)}, u32[]{:S(2)}, u32[]{:S(2)}) %collective-permute-start.3) | collective-permute-done | bytes 135200 | tf_op jit(solution)/shard_map/ppermute | solution.py:384
  32.4 4.9 %collective-permute-start.6 = (bf16[528,128]{1,0:T(8,128)(2,1)S(1)}, bf16[528,128]{1,0:T(8,128)(2,1)S(1)}, u32[]{:S(2)}, u32[]{:S(2)}) collective-permute-start(bf16[528,128]{1,0:T(8,128)(2,1)S(1)} %collective-permute-done.3.refs_1_.refs_0_), channel_id=1, source_target_pairs={{0,32},{1,97},{16,48},{17,113},{32,64},{33,1},{48,80},{49,17},{64,... | collective-permute-start | bytes 405512 | tf_op jit(solution)/shard_map/ppermute | solution.py:384
  37.3 3.0 %collective-permute-done.6.refs_2_.refs_0_ = bf16[528,128]{1,0:T(8,128)(2,1)S(1)} collective-permute-done((bf16[528,128]{1,0:T(8,128)(2,1)S(1)}, bf16[528,128]{1,0:T(8,128)(2,1)S(1)}, u32[]{:S(2)}, u32[]{:S(2)}) %collective-permute-start.6) | collective-permute-done | bytes 135200 | tf_op jit(solution)/shard_map/ppermute | solution.py:384
  40.5 5.8 %collective-permute-start.8 = (bf16[2112,128]{1,0:T(8,128)(2,1)S(1)}, bf16[2112,128]{1,0:T(8,128)(2,1)S(1)}, u32[]{:S(2)}, u32[]{:S(2)}) collective-permute-start(bf16[2112,128]{1,0:T(8,128)(2,1)S(1)} %collective-permute-done.4.refs_6_), channel_id=1, source_target_pairs={{0,1},{1,0},{2,3},{3,2},{4,5},{5,4},{6,7},{7,6},{8,9},{9,8},{10,11... | collective-permute-start | bytes 1622024 | tf_op jit(solution)/shard_map/ppermute | solution.py:412
  46.3 4.2 %collective-permute-done.10.refs_10_ = bf16[2112,128]{1,0:T(8,128)(2,1)S(1)} collective-permute-done((bf16[2112,128]{1,0:T(8,128)(2,1)S(1)}, bf16[2112,128]{1,0:T(8,128)(2,1)S(1)}, u32[]{:S(2)}, u32[]{:S(2)}) %collective-permute-start.10) | collective-permute-done | bytes 540704 | tf_op jit(solution)/shard_map/ppermute | solution.py:407
  50.5 4.7 %collective-permute-start.11 = (bf16[2112,128]{1,0:T(8,128)(2,1)S(1)}, bf16[2112,128]{1,0:T(8,128)(2,1)S(1)}, u32[]{:S(2)}, u32[]{:S(2)}) collective-permute-start(bf16[2112,128]{1,0:T(8,128)(2,1)S(1)} %collective-permute-done.10.refs_10_), channel_id=1, source_target_pairs={{0,1},{1,0},{2,3},{3,2},{4,5},{5,4},{6,7},{7,6},{8,9},{9,8},{10,11... | collective-permute-start | bytes 1622024 | tf_op jit(solution)/shard_map/ppermute | solution.py:412
  58.9 2.5 %assemble.1 = (bf16[4,2112,128]{2,1,0:T(8,128)(2,1)S(1)}, bf16[4,2112,128]{2,1,0:T(8,128)(2,1)S(1)}, s32[12]{0:T(128)S(1)}) custom-call(s32[4]{0:T(128)S(1)} %copy-done.3, s32[1]{0:T(128)S(6)} %copy.26.start, bf16[528,128]{1,0:T(8,128)(2,1)S(1)} %payload.1.refs_0_, bf16[528,128]{1,0:T(8,128)(2,1)S(1)} %collective-permute-done.3.refs_1_.refs_0_, ...), custom_call_target="tpu_custom_call" | custom-call | tf_op jit(solution)/shard_map/assemble/pallas_call | solution.py:162
  61.4 7.3 %attend.4 = (bf16[544,128]{1,0:T(8,128)(2,1)S(1)}, s32[12]{0:T(128)S(1)}) custom-call(s32[12]{0:T(128)S(1)} %get-tuple-element.34.meta, bf16[528,128]{1,0:T(8,128)(2,1)S(1)} %collective-permute-done.6.refs_2_.refs_0_, bf16[4,2112,128]{2,1,0:T(8,128)(2,1)S(1)} %get-tuple-element.35.refs_1_, bf16[4,2112,128]{2,1,0:T(8,128)(2,1)S(1)} %get-tuple-element.36.refs_2_), custom_call_target="tpu_custom_call" | custom-call | flops 600000000 | bytes 100000 | tf_op jit(solution)/shard_map/attend/pallas_call | solution.py:321
  68.7 1.2 collective-permute-start.12
  69.9 7.3 %attend.5 = (bf16[544,128]{1,0:T(8,128)(2,1)S(1)}, s32[12]{0:T(128)S(1)}) custom-call(s32[12]{0:T(128)S(1)} %get-tuple-element.37.meta, bf16[528,128]{1,0:T(8,128)(2,1)S(1)} %collective-permute-done.3.refs_1_.refs_0_, bf16[4,2112,128]{2,1,0:T(8,128)(2,1)S(1)} %get-tuple-element.35.refs_1_, bf16[4,2112,128]{2,1,0:T(8,128)(2,1)S(1)} %get-tuple-element.36.refs_2_), custom_call_target="tpu_custom_call" | custom-call | flops 600000000 | bytes 100000 | tf_op jit(solution)/shard_map/attend/pallas_call | solution.py:321
  77.3 3.1 %collective-permute-start.15 = (bf16[544,128]{1,0:T(8,128)(2,1)S(1)}, bf16[544,128]{1,0:T(8,128)(2,1)S(1)}, u32[]{:S(2)}, u32[]{:S(2)}) collective-permute-start(bf16[544,128]{1,0:T(8,128)(2,1)S(1)} %get-tuple-element.45), channel_id=1, source_target_pairs={{0,96},{1,33},{16,112},{17,49},{32,0},{33,65},{48,16},{49,81},{64,... | collective-permute-start | bytes 417800 | tf_op jit(solution)/shard_map/ppermute | solution.py:384
  80.4 7.3 %attend.6 = (bf16[544,128]{1,0:T(8,128)(2,1)S(1)}, s32[12]{0:T(128)S(1)}) custom-call(s32[12]{0:T(128)S(1)} %get-tuple-element.38.meta, bf16[528,128]{1,0:T(8,128)(2,1)S(1)} %collective-permute-done.7.refs_3_.refs_0_, bf16[4,2112,128]{2,1,0:T(8,128)(2,1)S(1)} %get-tuple-element.35.refs_1_, bf16[4,2112,128]{2,1,0:T(8,128)(2,1)S(1)} %get-tuple-element.36.refs_2_, ...), custom_call_target="tpu_custom_call" | custom-call | flops 600000000 | bytes 100000 | tf_op jit(solution)/shard_map/attend/pallas_call | solution.py:321
  87.8 7.3 %attend.7 = (bf16[544,128]{1,0:T(8,128)(2,1)S(1)}, s32[12]{0:T(128)}) custom-call(s32[12]{0:T(128)S(1)} %get-tuple-element.40.meta, bf16[528,128]{1,0:T(8,128)(2,1)S(1)} %payload.1.refs_0_, bf16[4,2112,128]{2,1,0:T(8,128)(2,1)S(1)} %get-tuple-element.35.refs_1_, bf16[4,2112,128]{2,1,0:T(8,128)(2,1)S(1)} %get-tuple-element.36.refs_2_), custom_call_target="tpu_custom_call" | custom-call | flops 600000000 | bytes 100000 | tf_op jit(solution)/shard_map/attend/pallas_call | solution.py:321
  95.1 1.7 %combine.1 = (bf16[512,128]{1,0:T(8,128)(2,1)}, bf16[16,1024]{1,0:T(8,128)(2,1)S(1)}, bf16[16,1024]{1,0:T(8,128)(2,1)S(1)}, bf16[16,1024]{1,0:T(8,128)(2,1)S(1)}, bf16[16,1024]{1,0:T(8,128)(2,1)S(1)}) custom-call(s32[4]{0:T(128)S(1)} %copy-done.3, bf16[544,128]{1,0:T(8,128)(2,1)S(1)} %get-tuple-element.43.refs_0_, ...), custom_call_target="tpu_custom_call" | custom-call | tf_op jit(solution)/shard_map/combine/pallas_call | solution.py:365
  96.8 3.5 %collective-permute-start.16 = (bf16[16,1024]{1,0:T(8,128)(2,1)S(1)}, bf16[16,1024]{1,0:T(8,128)(2,1)S(1)}, u32[]{:S(2)}, u32[]{:S(2)}) collective-permute-start(bf16[16,1024]{1,0:T(8,128)(2,1)S(1)} %get-tuple-element.48), channel_id=1, source_target_pairs={{0,1},{1,0},{2,3},{3,2},{4,5},{5,4},{6,7},{7,6},{8,9},{9,8},{10,11... | collective-permute-start | bytes 98312 | tf_op jit(solution)/shard_map/ppermute | solution.py:427
  100.3 1.6 %collective-permute-start.18 = (bf16[16,1024]{1,0:T(8,128)(2,1)S(1)}, bf16[16,1024]{1,0:T(8,128)(2,1)S(1)}, u32[]{:S(2)}, u32[]{:S(2)}) collective-permute-start(bf16[16,1024]{1,0:T(8,128)(2,1)S(1)} %get-tuple-element.50), channel_id=1, source_target_pairs={{0,129},{1,128},{128,1},{129,0},{2,131},{3,130},{130,3},{131,2},{4... | collective-permute-start | bytes 98312 | tf_op jit(solution)/shard_map/ppermute | solution.py:429
  104.3 1.5 collective-permute-start.20
  105.9 2.2 %collective-permute-done.19 = bf16[2,1,16,2048]{3,2,0,1:T(8,128)(2,1)S(1)} collective-permute-done((bf16[2,1,16,2048]{3,2,0,1:T(8,128)(2,1)S(1)}, bf16[2,1,16,2048]{3,2,0,1:T(8,128)(2,1)S(1)}, u32[]{:S(2)}, u32[]{:S(2)}) %collective-permute-start.19) | collective-permute-done | bytes 131104 | tf_op jit(solution)/shard_map/ppermute | solution.py:384
  108.1 1.2 collective-permute-start.21
  110.4 1.7 %collective-permute-done.21 = bf16[2,1,16,2048]{3,2,0,1:T(8,128)(2,1)S(1)} collective-permute-done((bf16[2,1,16,2048]{3,2,0,1:T(8,128)(2,1)S(1)}, bf16[2,1,16,2048]{3,2,0,1:T(8,128)(2,1)S(1)}, u32[]{:S(2)}, u32[]{:S(2)}) %collective-permute-start.21) | collective-permute-done | bytes 131104 | tf_op jit(solution)/shard_map/ppermute | solution.py:384
  112.2 2.3 %collective-permute-start.23 = (bf16[2,1,16,2048]{3,2,0,1:T(8,128)(2,1)S(1)}, bf16[2,1,16,2048]{3,2,0,1:T(8,128)(2,1)S(1)}, u32[]{:S(2)}, u32[]{:S(2)}) collective-permute-start(bf16[2,1,16,2048]{3,2,0,1:T(8,128)(2,1)S(1)} %collective-permute-done.21), channel_id=1, source_target_pairs={{0,16},{1,113},{16,32},{17,1},{32,48},{33,17},{48,64},{49,33},{64,... | collective-permute-start | bytes 393224 | tf_op jit(solution)/shard_map/ppermute | solution.py:384
  115.5 2.5 %collective-permute-done.23 = bf16[2,1,16,2048]{3,2,0,1:T(8,128)(2,1)S(1)} collective-permute-done((bf16[2,1,16,2048]{3,2,0,1:T(8,128)(2,1)S(1)}, bf16[2,1,16,2048]{3,2,0,1:T(8,128)(2,1)S(1)}, u32[]{:S(2)}, u32[]{:S(2)}) %collective-permute-start.23) | collective-permute-done | bytes 131104 | tf_op jit(solution)/shard_map/ppermute | solution.py:384
  118.0 2.8 %collective-permute-start.25 = (bf16[2,1,16,2048]{3,2,0,1:T(8,128)(2,1)S(1)}, bf16[2,1,16,2048]{3,2,0,1:T(8,128)(2,1)S(1)}, u32[]{:S(2)}, u32[]{:S(2)}) collective-permute-start(bf16[2,1,16,2048]{3,2,0,1:T(8,128)(2,1)S(1)} %collective-permute-done.23), channel_id=1, source_target_pairs={{0,16},{1,113},{16,32},{17,1},{32,48},{33,17},{48,64},{49,33},{64,... | collective-permute-start | bytes 393224 | tf_op jit(solution)/shard_map/ppermute | solution.py:384
  120.9 1.9 %collective-permute-done.25 = bf16[2,1,16,2048]{3,2,0,1:T(8,128)(2,1)S(1)} collective-permute-done((bf16[2,1,16,2048]{3,2,0,1:T(8,128)(2,1)S(1)}, bf16[2,1,16,2048]{3,2,0,1:T(8,128)(2,1)S(1)}, u32[]{:S(2)}, u32[]{:S(2)}) %collective-permute-start.25) | collective-permute-done | bytes 131104 | tf_op jit(solution)/shard_map/ppermute | solution.py:384
  126.6 31.9 %all_to_all.5 = bf16[32,16,1024]{2,1,0:T(8,128)(2,1)S(1)} all-to-all(bf16[32,16,1024]{2,1,0:T(8,128)(2,1)S(1)} %bitcast.47), channel_id=1, replica_groups=mesh['xl'=2,'z'=8,'y'=4,'xh'=2,'core'=2] {'xl','y','xh','core'}, dimensions={0} | all-to-all | bytes 2097152 | tf_op jit(solution)/shard_map/all_to_all | solution.py:450
  (65 shorter events, 13.4 us)
Async XLA Ops:
  1.2 20.3 %copy-start.2 = (bf16[64,8,128]{2,1,0:T(8,128)(2,1)S(1)}, bf16[64,8,128]{2,1,0:T(8,128)(2,1)}, u32[]{:S(2)}) copy-start(bf16[64,8,128]{2,1,0:T(8,128)(2,1)} %param.8) | copy-start | bytes 393220
  1.2 39.1 %copy-start.4 = (bf16[1024,1024]{1,0:T(8,128)(2,1)S(1)}, bf16[1024,1024]{1,0:T(8,128)(2,1)}, u32[]{:S(2)}) copy-start(bf16[1024,1024]{1,0:T(8,128)(2,1)} %param.15) | copy-start | bytes 6291460
  1.2 55.6 %copy-start.3 = (s32[4]{0:T(128)S(1)}, s32[4]{0:T(128)}, u32[]{:S(2)}) copy-start(s32[4]{0:T(128)} %pad_add_fusion.place) | copy-start | bytes 52
  4.6 35.7 %collective-permute-start.5 = (bf16[2112,128]{1,0:T(8,128)(2,1)}, bf16[2112,128]{1,0:T(8,128)(2,1)S(1)}, u32[]{:S(2)}, u32[]{:S(2)}) collective-permute-start(bf16[2112,128]{1,0:T(8,128)(2,1)} %get-tuple-element.28.refs_4_), channel_id=1, source_target_pairs={{0,16},{16,0},{32,48},{48,32},{64,80},{80,64},{96,112},{112,96},{1... | collective-permute-start | bytes 1622024 | tf_op jit(solution)/shard_map/ppermute | solution.py:392
  7.2 33.1 %collective-permute-start.4 = (bf16[2112,128]{1,0:T(8,128)(2,1)}, bf16[2112,128]{1,0:T(8,128)(2,1)S(1)}, u32[]{:S(2)}, u32[]{:S(2)}) collective-permute-start(bf16[2112,128]{1,0:T(8,128)(2,1)} %get-tuple-element.27), channel_id=1, source_target_pairs={{0,130},{2,128},{128,2},{130,0},{1,131},{3,129},{129,3},{131,1},{4... | collective-permute-start | bytes 1622024 | tf_op jit(solution)/shard_map/ppermute | solution.py:391
  9.7 11.8 %collective-permute-start = (s32[1]{0:T(128)}, s32[1]{0:T(128)}, u32[]{:S(2)}, u32[]{:S(2)}) collective-permute-start(s32[1]{0:T(128)} %param.14), channel_id=1, source_target_pairs={{0,130},{2,128},{128,2},{130,0},{1,131},{3,129},{129,3},{131,1},{4... | collective-permute-start | bytes 20 | tf_op jit(solution)/shard_map/ppermute | solution.py:397
  9.9 11.6 %collective-permute-start.1 = (s32[1]{0:T(128)}, s32[1]{0:T(128)}, u32[]{:S(2)}, u32[]{:S(2)}) collective-permute-start(s32[1]{0:T(128)} %param.14), channel_id=1, source_target_pairs={{0,16},{16,0},{32,48},{48,32},{64,80},{80,64},{96,112},{112,96},{1... | collective-permute-start | bytes 20 | tf_op jit(solution)/shard_map/ppermute | solution.py:398
  10.0 11.5 %collective-permute-start.2 = (s32[1]{0:T(128)}, s32[1]{0:T(128)}, u32[]{:S(2)}, u32[]{:S(2)}) collective-permute-start(s32[1]{0:T(128)} %param.14), channel_id=1, source_target_pairs={{0,146},{2,144},{16,130},{18,128},{32,178},{34,176},{48,162},{50,1... | collective-permute-start | bytes 20 | tf_op jit(solution)/shard_map/ppermute | solution.py:399
  23.4 9.0 %collective-permute-start.3 = (bf16[528,128]{1,0:T(8,128)(2,1)S(1)}, bf16[528,128]{1,0:T(8,128)(2,1)S(1)}, u32[]{:S(2)}, u32[]{:S(2)}) collective-permute-start(bf16[528,128]{1,0:T(8,128)(2,1)S(1)} %payload.1.refs_0_), channel_id=1, source_target_pairs={{0,32},{1,97},{16,48},{17,113},{32,64},{33,1},{48,80},{49,17},{64,... | collective-permute-start | bytes 405512 | tf_op jit(solution)/shard_map/ppermute | solution.py:384
  28.8 8.5 %collective-permute-start.7 = (bf16[528,128]{1,0:T(8,128)(2,1)S(1)}, bf16[528,128]{1,0:T(8,128)(2,1)S(1)}, u32[]{:S(2)}, u32[]{:S(2)}) collective-permute-start(bf16[528,128]{1,0:T(8,128)(2,1)S(1)} %payload.1.refs_0_), channel_id=1, source_target_pairs={{0,96},{1,33},{16,112},{17,49},{32,0},{33,65},{48,16},{49,81},{64,... | collective-permute-start | bytes 405512 | tf_op jit(solution)/shard_map/ppermute | solution.py:384
  32.4 7.9 %collective-permute-start.6 = (bf16[528,128]{1,0:T(8,128)(2,1)S(1)}, bf16[528,128]{1,0:T(8,128)(2,1)S(1)}, u32[]{:S(2)}, u32[]{:S(2)}) collective-permute-start(bf16[528,128]{1,0:T(8,128)(2,1)S(1)} %collective-permute-done.3.refs_1_.refs_0_), channel_id=1, source_target_pairs={{0,32},{1,97},{16,48},{17,113},{32,64},{33,1},{48,80},{49,17},{64,... | collective-permute-start | bytes 405512 | tf_op jit(solution)/shard_map/ppermute | solution.py:384
  40.3 54.7 %collective-permute-start.13 = (bf16[1024,1024]{1,0:T(8,128)(2,1)S(1)}, bf16[1024,1024]{1,0:T(8,128)(2,1)S(1)}, u32[]{:S(2)}, u32[]{:S(2)}) collective-permute-start(bf16[1024,1024]{1,0:T(8,128)(2,1)S(1)} %copy-done.4), channel_id=1, source_target_pairs={{0,128},{128,0},{1,129},{129,1},{2,130},{130,2},{3,131},{131,3},{4... | collective-permute-start | bytes 6291464 | tf_op jit(solution)/shard_map/ppermute | solution.py:408
  40.4 10.1 %collective-permute-start.10 = (bf16[2112,128]{1,0:T(8,128)(2,1)S(1)}, bf16[2112,128]{1,0:T(8,128)(2,1)S(1)}, u32[]{:S(2)}, u32[]{:S(2)}) collective-permute-start(bf16[2112,128]{1,0:T(8,128)(2,1)S(1)} %collective-permute-done.4.refs_6_), channel_id=1, source_target_pairs={{0,16},{16,0},{32,48},{48,32},{64,80},{80,64},{96,112},{112,96},{1... | collective-permute-start | bytes 1622024 | tf_op jit(solution)/shard_map/ppermute | solution.py:407
  40.5 15.3 %collective-permute-start.8 = (bf16[2112,128]{1,0:T(8,128)(2,1)S(1)}, bf16[2112,128]{1,0:T(8,128)(2,1)S(1)}, u32[]{:S(2)}, u32[]{:S(2)}) collective-permute-start(bf16[2112,128]{1,0:T(8,128)(2,1)S(1)} %collective-permute-done.4.refs_6_), channel_id=1, source_target_pairs={{0,1},{1,0},{2,3},{3,2},{4,5},{5,4},{6,7},{7,6},{8,9},{9,8},{10,11... | collective-permute-start | bytes 1622024 | tf_op jit(solution)/shard_map/ppermute | solution.py:412
  46.3 9.6 %collective-permute-start.9 = (bf16[2112,128]{1,0:T(8,128)(2,1)S(1)}, bf16[2112,128]{1,0:T(8,128)(2,1)S(1)}, u32[]{:S(2)}, u32[]{:S(2)}) collective-permute-start(bf16[2112,128]{1,0:T(8,128)(2,1)S(1)} %collective-permute-done.5.refs_8_), channel_id=1, source_target_pairs={{0,1},{1,0},{2,3},{3,2},{4,5},{5,4},{6,7},{7,6},{8,9},{9,8},{10,11... | collective-permute-start | bytes 1622024 | tf_op jit(solution)/shard_map/ppermute | solution.py:412
  50.5 6.2 %collective-permute-start.11 = (bf16[2112,128]{1,0:T(8,128)(2,1)S(1)}, bf16[2112,128]{1,0:T(8,128)(2,1)S(1)}, u32[]{:S(2)}, u32[]{:S(2)}) collective-permute-start(bf16[2112,128]{1,0:T(8,128)(2,1)S(1)} %collective-permute-done.10.refs_10_), channel_id=1, source_target_pairs={{0,1},{1,0},{2,3},{3,2},{4,5},{5,4},{6,7},{7,6},{8,9},{9,8},{10,11... | collective-permute-start | bytes 1622024 | tf_op jit(solution)/shard_map/ppermute | solution.py:412
  68.7 11.6 %collective-permute-start.12 = (bf16[544,128]{1,0:T(8,128)(2,1)S(1)}, bf16[544,128]{1,0:T(8,128)(2,1)S(1)}, u32[]{:S(2)}, u32[]{:S(2)}) collective-permute-start(bf16[544,128]{1,0:T(8,128)(2,1)S(1)} %get-tuple-element.39), channel_id=1, source_target_pairs={{0,32},{1,97},{16,48},{17,113},{32,64},{33,1},{48,80},{49,17},{64,... | collective-permute-start | bytes 417800 | tf_op jit(solution)/shard_map/ppermute | solution.py:384
  77.3 17.8 %collective-permute-start.15 = (bf16[544,128]{1,0:T(8,128)(2,1)S(1)}, bf16[544,128]{1,0:T(8,128)(2,1)S(1)}, u32[]{:S(2)}, u32[]{:S(2)}) collective-permute-start(bf16[544,128]{1,0:T(8,128)(2,1)S(1)} %get-tuple-element.45), channel_id=1, source_target_pairs={{0,96},{1,33},{16,112},{17,49},{32,0},{33,65},{48,16},{49,81},{64,... | collective-permute-start | bytes 417800 | tf_op jit(solution)/shard_map/ppermute | solution.py:384
  87.7 7.4 %collective-permute-start.14 = (bf16[544,128]{1,0:T(8,128)(2,1)S(1)}, bf16[544,128]{1,0:T(8,128)(2,1)S(1)}, u32[]{:S(2)}, u32[]{:S(2)}) collective-permute-start(bf16[544,128]{1,0:T(8,128)(2,1)S(1)} %get-tuple-element.44), channel_id=1, source_target_pairs={{0,32},{1,97},{16,48},{17,113},{32,64},{33,1},{48,80},{49,17},{64,... | collective-permute-start | bytes 417800 | tf_op jit(solution)/shard_map/ppermute | solution.py:384
  95.1 5.2 %copy-start.5 = (bf16[1024,1024]{1,0:T(8,128)(2,1)}, bf16[1024,1024]{1,0:T(8,128)(2,1)S(1)}, u32[]{:S(2)}) copy-start(bf16[1024,1024]{1,0:T(8,128)(2,1)S(1)} %collective-permute-done.13) | copy-start | bytes 6291460
  96.8 5.7 %collective-permute-start.16 = (bf16[16,1024]{1,0:T(8,128)(2,1)S(1)}, bf16[16,1024]{1,0:T(8,128)(2,1)S(1)}, u32[]{:S(2)}, u32[]{:S(2)}) collective-permute-start(bf16[16,1024]{1,0:T(8,128)(2,1)S(1)} %get-tuple-element.48), channel_id=1, source_target_pairs={{0,1},{1,0},{2,3},{3,2},{4,5},{5,4},{6,7},{7,6},{8,9},{9,8},{10,11... | collective-permute-start | bytes 98312 | tf_op jit(solution)/shard_map/ppermute | solution.py:427
  100.3 2.8 %collective-permute-start.17 = (bf16[16,1024]{1,0:T(8,128)(2,1)S(1)}, bf16[16,1024]{1,0:T(8,128)(2,1)S(1)}, u32[]{:S(2)}, u32[]{:S(2)}) collective-permute-start(bf16[16,1024]{1,0:T(8,128)(2,1)S(1)} %get-tuple-element.49), channel_id=1, source_target_pairs={{0,128},{128,0},{1,129},{129,1},{2,130},{130,2},{3,131},{131,3},{4... | collective-permute-start | bytes 98312 | tf_op jit(solution)/shard_map/ppermute | solution.py:428
  100.3 3.8 %collective-permute-start.18 = (bf16[16,1024]{1,0:T(8,128)(2,1)S(1)}, bf16[16,1024]{1,0:T(8,128)(2,1)S(1)}, u32[]{:S(2)}, u32[]{:S(2)}) collective-permute-start(bf16[16,1024]{1,0:T(8,128)(2,1)S(1)} %get-tuple-element.50), channel_id=1, source_target_pairs={{0,129},{1,128},{128,1},{129,0},{2,131},{3,130},{130,3},{131,2},{4... | collective-permute-start | bytes 98312 | tf_op jit(solution)/shard_map/ppermute | solution.py:429
  101.9 20.8 %collective-permute-start.26 = (bf16[1024,1024]{1,0:T(8,128)(2,1)S(1)}, bf16[1024,1024]{1,0:T(8,128)(2,1)S(1)}, u32[]{:S(2)}, u32[]{:S(2)}) collective-permute-start(bf16[1024,1024]{1,0:T(8,128)(2,1)S(1)} %copy-done.4), channel_id=1, source_target_pairs={{0,1},{1,0},{2,3},{3,2},{4,5},{5,4},{6,7},{7,6},{8,9},{9,8},{10,11... | collective-permute-start | bytes 6291464 | tf_op jit(solution)/shard_map/ppermute | solution.py:409
  102.2 21.3 %collective-permute-start.27 = (bf16[1024,1024]{1,0:T(8,128)(2,1)}, bf16[1024,1024]{1,0:T(8,128)(2,1)S(1)}, u32[]{:S(2)}, u32[]{:S(2)}) collective-permute-start(bf16[1024,1024]{1,0:T(8,128)(2,1)} %copy-done.5), channel_id=1, source_target_pairs={{0,1},{1,0},{2,3},{3,2},{4,5},{5,4},{6,7},{7,6},{8,9},{9,8},{10,11... | collective-permute-start | bytes 6291464 | tf_op jit(solution)/shard_map/ppermute | solution.py:423
  104.2 3.9 %collective-permute-start.19 = (bf16[2,1,16,2048]{3,2,0,1:T(8,128)(2,1)S(1)}, bf16[2,1,16,2048]{3,2,0,1:T(8,128)(2,1)S(1)}, u32[]{:S(2)}, u32[]{:S(2)}) collective-permute-start(bf16[2,1,16,2048]{3,2,0,1:T(8,128)(2,1)S(1)} %fusion.8), channel_id=1, source_target_pairs={{0,16},{1,113},{16,32},{17,1},{32,48},{33,17},{48,64},{49,33},{64,... | collective-permute-start | bytes 393224 | tf_op jit(solution)/shard_map/ppermute | solution.py:384
  104.3 6.1 %collective-permute-start.20 = (bf16[2,1,16,2048]{3,2,0,1:T(8,128)(2,1)S(1)}, bf16[2,1,16,2048]{3,2,0,1:T(8,128)(2,1)S(1)}, u32[]{:S(2)}, u32[]{:S(2)}) collective-permute-start(bf16[2,1,16,2048]{3,2,0,1:T(8,128)(2,1)S(1)} %fusion.8), channel_id=1, source_target_pairs={{0,112},{1,17},{16,0},{17,33},{32,16},{33,49},{48,32},{49,65},{64,... | collective-permute-start | bytes 393224 | tf_op jit(solution)/shard_map/ppermute | solution.py:384
  108.1 4.1 %collective-permute-start.21 = (bf16[2,1,16,2048]{3,2,0,1:T(8,128)(2,1)S(1)}, bf16[2,1,16,2048]{3,2,0,1:T(8,128)(2,1)S(1)}, u32[]{:S(2)}, u32[]{:S(2)}) collective-permute-start(bf16[2,1,16,2048]{3,2,0,1:T(8,128)(2,1)S(1)} %collective-permute-done.19), channel_id=1, source_target_pairs={{0,16},{1,113},{16,32},{17,1},{32,48},{33,17},{48,64},{49,33},{64,... | collective-permute-start | bytes 393224 | tf_op jit(solution)/shard_map/ppermute | solution.py:384
  110.4 5.0 %collective-permute-start.22 = (bf16[2,1,16,2048]{3,2,0,1:T(8,128)(2,1)S(1)}, bf16[2,1,16,2048]{3,2,0,1:T(8,128)(2,1)S(1)}, u32[]{:S(2)}, u32[]{:S(2)}) collective-permute-start(bf16[2,1,16,2048]{3,2,0,1:T(8,128)(2,1)S(1)} %collective-permute-done.20), channel_id=1, source_target_pairs={{0,112},{1,17},{16,0},{17,33},{32,16},{33,49},{48,32},{49,65},{64,... | collective-permute-start | bytes 393224 | tf_op jit(solution)/shard_map/ppermute | solution.py:384
  112.2 5.8 %collective-permute-start.23 = (bf16[2,1,16,2048]{3,2,0,1:T(8,128)(2,1)S(1)}, bf16[2,1,16,2048]{3,2,0,1:T(8,128)(2,1)S(1)}, u32[]{:S(2)}, u32[]{:S(2)}) collective-permute-start(bf16[2,1,16,2048]{3,2,0,1:T(8,128)(2,1)S(1)} %collective-permute-done.21), channel_id=1, source_target_pairs={{0,16},{1,113},{16,32},{17,1},{32,48},{33,17},{48,64},{49,33},{64,... | collective-permute-start | bytes 393224 | tf_op jit(solution)/shard_map/ppermute | solution.py:384
  115.4 5.4 %collective-permute-start.24 = (bf16[2,1,16,2048]{3,2,0,1:T(8,128)(2,1)S(1)}, bf16[2,1,16,2048]{3,2,0,1:T(8,128)(2,1)S(1)}, u32[]{:S(2)}, u32[]{:S(2)}) collective-permute-start(bf16[2,1,16,2048]{3,2,0,1:T(8,128)(2,1)S(1)} %collective-permute-done.22), channel_id=1, source_target_pairs={{0,112},{1,17},{16,0},{17,33},{32,16},{33,49},{48,32},{49,65},{64,... | collective-permute-start | bytes 393224 | tf_op jit(solution)/shard_map/ppermute | solution.py:384
  118.0 4.8 %collective-permute-start.25 = (bf16[2,1,16,2048]{3,2,0,1:T(8,128)(2,1)S(1)}, bf16[2,1,16,2048]{3,2,0,1:T(8,128)(2,1)S(1)}, u32[]{:S(2)}, u32[]{:S(2)}) collective-permute-start(bf16[2,1,16,2048]{3,2,0,1:T(8,128)(2,1)S(1)} %collective-permute-done.23), channel_id=1, source_target_pairs={{0,16},{1,113},{16,32},{17,1},{32,48},{33,17},{48,64},{49,33},{64,... | collective-permute-start | bytes 393224 | tf_op jit(solution)/shard_map/ppermute | solution.py:384
  (3 other events, 3.7 us)
